TPU v7x, 32 devices: a whole 2x2x4 slice. The times are simulated.
32 devices in a mesh: dp: 8 (over z, y), head: 4 (over x, core).
Axes of the slice: x: 2, y: 2, z: 4, core: 2. Of those that a mesh axis runs over, the one named last changes fastest.
Arguments:
- features: bfloat16 [32768, 768], P('dp'), may hold values from -6 to 6
- laplacian: float32 [8192, 16], P('dp'), may hold values from -4 to 4
- endpoints: int32 [32768, 2], P('dp'), may hold values from 0 to 31
- lengths: int32 [16, 16], P('dp'), may hold values from 1 to 128, 1536 in all within a row
- pairing: int32 [8, 16], P('dp'), may hold values from 0 to 15, each once within a row
- ident_weight: float32 [32, 768], P(None, ('dp', 'head')), may hold values from -1 to 1
- qkv_weight: float32 [768, 3, 768], P('dp', None, 'head'), may hold values from -0.21875 to 0.21875
- out_weight: float32 [768, 768], P('head', 'dp'), may hold values from -1.75 to 1.75
- ffn_weight: float32 [2, 768, 768], P(None, ('dp', 'head')), may hold values from -0.21875 to 0.21875
- norm_gains: float32 [3, 768], P(None, ('dp', 'head')), may hold values from 0.5 to 1.5
- ident_first: float32 [32, 768], P(None, ('dp', 'head')), may hold values from -0.015625 to 0.015625
- qkv_first: float32 [768, 3, 768], P('dp', None, 'head'), may hold values from -0.015625 to 0.015625
- out_first: float32 [768, 768], P('head', 'dp'), may hold values from -0.015625 to 0.015625
- ffn_first: float32 [2, 768, 768], P(None, ('dp', 'head')), may hold values from -0.015625 to 0.015625
- gains_first: float32 [3, 768], P(None, ('dp', 'head')), may hold values from -0.0625 to 0.0625
- ident_second: float32 [32, 768], P(None, ('dp', 'head')), may hold values from 7.0110023e-06 to 2.8044009e-05
- qkv_second: float32 [768, 3, 768], P('dp', None, 'head'), may hold values from 7.0110023e-06 to 2.8044009e-05
- out_second: float32 [768, 768], P('head', 'dp'), may hold values from 7.0110023e-06 to 2.8044009e-05
- ffn_second: float32 [2, 768, 768], P(None, ('dp', 'head')), may hold values from 7.0110023e-06 to 2.8044009e-05
- gains_second: float32 [3, 768], P(None, ('dp', 'head')), may hold values from 0.000112176036 to 0.00044870414
Outputs:
- grad_norm: float32 [], replicated
- total_loss: float32 [], replicated
- new_ident: float32 [32, 768], P(None, ('dp', 'head'))
- new_qkv: float32 [768, 3, 768], P('dp', None, 'head')
- new_out: float32 [768, 768], P('head', 'dp')
- new_ffn: float32 [2, 768, 768], P(None, ('dp', 'head'))
- new_gains: float32 [3, 768], P(None, ('dp', 'head'))
- first_ident: float32 [32, 768], P(None, ('dp', 'head'))
- first_qkv: float32 [768, 3, 768], P('dp', None, 'head')
- first_out: float32 [768, 768], P('head', 'dp')
- first_ffn: float32 [2, 768, 768], P(None, ('dp', 'head'))
- first_gains: float32 [3, 768], P(None, ('dp', 'head'))
- second_ident: float32 [32, 768], P(None, ('dp', 'head'))
- second_qkv: float32 [768, 3, 768], P('dp', None, 'head')
- second_out: float32 [768, 768], P('head', 'dp')
- second_ffn: float32 [2, 768, 768], P(None, ('dp', 'head'))
- second_gains: float32 [3, 768], P(None, ('dp', 'head'))
All inputs are finite; a program needn't handle non-finite values.
Results may differ from a plain program's by a relative error of at most 0.0099.
Values may be sent and summed in bfloat16 or wider, within the bound.
No kernel may reach another device: no remote copies, remote signals or barrier semaphores. Data moves between devices by JAX's collectives and lax.ppermute only.
A program may use at most 192 MiB of HBM per device.

v0:
```python
import functools

import jax
import jax.numpy as jnp
from jax import lax
from jax.experimental import pallas as pl
from jax.experimental.pallas import tpu as pltpu
from jax.sharding import PartitionSpec as P

D = 768
HEAD_DIM = 24
LAP = 16
LEN = 128
NODE = 32
STEPS = 3
GRAPHS_DEV = 16
GAIN = 2 * LAP

HIGHEST = lax.Precision.HIGHEST
NORM_EPS = 1e-05
CLIP_AT = 5.0
STEP_RATES = (0.08, 0.02, 0.15, 0.02, 0.5)
BETA_ONE = 0.5
BETA_TWO = 0.5
DECAY = 0.01
ADAM_EPS = 1e-08
MASKED = -1e30

BF = jnp.bfloat16
F32 = jnp.float32
SUB = 4
SW = SUB * HEAD_DIM
PACK = 4 * SW
V_AT = 128 - SW
SCALE = HEAD_DIM ** (-0.5)
LENS = 5
VMEM_LIMIT = 52 * 2**20


def nn(a, b):
    return lax.dot_general(a, b, (((1,), (0,)), ((), ())), preferred_element_type=F32)


def nt(a, b):
    return lax.dot_general(a, b, (((1,), (1,)), ((), ())), preferred_element_type=F32)


def tn(a, b):
    return lax.dot_general(a, b, (((0,), (0,)), ((), ())), preferred_element_type=F32)


def lanes():
    return lax.broadcasted_iota(jnp.int32, (1, 128), 1)


def head_lanes(h, at):
    lane = lanes()
    return (lane >= at + h * HEAD_DIM) & (lane < at + (h + 1) * HEAD_DIM)


def by_head(v, at):
    zero = jnp.zeros_like(v)
    return jnp.concatenate([jnp.where(head_lanes(h, at), v, zero) for h in range(SUB)], axis=0)


def stack_heads(v):
    return jnp.concatenate([v[:, h * LEN : (h + 1) * LEN] for h in range(SUB)], axis=0)


def attend_kernel(info_ref, x_ref, *refs, graphs, whole, turn, owner):
    refs, turned = (refs[:-1], refs[-1:]) if turn else (refs, ())
    if whole:
        w_ref, qkv_ref, p_ref, o_ref, rinv_ref = refs
    else:
        first_ref, third_ref, w_ref, qkv_ref, p_ref, o_ref, rinv_ref = refs
        outs, rows = first_ref.shape[1], first_ref.shape[3]
        far, head = pl.program_id(0) // 2, pl.program_id(0) % 2
        outer, inner, gatherer = info_ref[0], info_ref[1], info_ref[owner]
        for i in range(2):
            in_first = (far == 0) if i == 0 else (far == 0) & (gatherer == 0)
            in_first = in_first | ((far == 1) & (gatherer == 1) & (i == 0))
            at = jnp.where(in_first, jnp.where(far + i == 0, 0, 1), jnp.where(far + i == 2, 1, 0))

            def place(source, at=at, i=i):
                for o in range(outs):
                    row = (lax.rem(outer + outs - o, outs) * 2 + (inner + i) % 2) * rows
                    w_ref[0, pl.ds(pl.multiple_of(row, rows), rows), :] = source[at, o, head]

            @pl.when(in_first)
            def _(place=place):
                place(first_ref)

            @pl.when(jnp.logical_not(in_first))
            def _(place=place):
                place(third_ref)

    if turned:

        @pl.when(pl.program_id(0) == 0)
        def _():
            turned[0][...] = x_ref[...].T

    y = nn(x_ref[...], w_ref[0])
    qkv_ref[0, 0] = y[:, :128].astype(BF)
    qkv_ref[0, 1] = pltpu.roll(y, PACK - SW, 1)[:, :128].astype(BF)
    qkv_ref[0, 2] = pltpu.roll(y, SW, 1)[:, 256:].astype(BF)
    col = lanes()
    ones = by_head(jnp.ones((LEN, 128), BF), V_AT)
    for g in range(graphs):
        rows = slice(g * LEN, (g + 1) * LEN)
        query, keys, values = qkv_ref[0, 0, rows, :], qkv_ref[0, 1, rows, :], qkv_ref[0, 2, rows, :]
        live = col < info_ref[LENS + g]
        scores = nt(query, by_head(keys, 0))
        parts = []
        for h in range(SUB):
            own = jnp.where(live, scores[:, h * LEN : (h + 1) * LEN] * SCALE, MASKED)
            parts.append(jnp.exp(own - jnp.max(own, axis=1, keepdims=True)).astype(BF))
        expo = jnp.concatenate(parts, axis=1)
        both = nn(expo, jnp.concatenate([by_head(values, V_AT), ones], axis=1))
        rinv = jnp.where(col >= V_AT, 1.0 / both[:, 128:], 0.0)
        p_ref[0, rows, :] = expo
        rinv_ref[0, rows, :] = rinv
        o_ref[0, rows, :] = jnp.where(col >= V_AT, both[:, :128] * rinv, 0.0).astype(BF)


def attend(info, owner, x, pieces, turn):
    tokens = x.shape[0]
    groups = 4
    whole = len(pieces) == 1
    block = lambda *tail: pl.BlockSpec((1,) + tail, lambda i: (i,) + (0,) * len(tail))
    full = lambda a: pl.BlockSpec(a.shape, lambda i: (0,) * a.ndim)
    out_specs = [block(3, tokens, 128), block(tokens, 512), block(tokens, 128), block(tokens, 128)]
    out_shape = [
        jax.ShapeDtypeStruct((groups, 3, tokens, 128), BF),
        jax.ShapeDtypeStruct((groups, tokens, 512), BF),
        jax.ShapeDtypeStruct((groups, tokens, 128), BF),
        jax.ShapeDtypeStruct((groups, tokens, 128), F32),
    ]
    if not whole:
        out_specs = [block(D, PACK)] + out_specs
        out_shape = [jax.ShapeDtypeStruct((groups, D, PACK), BF)] + out_shape
    if turn:
        out_specs = out_specs + [pl.BlockSpec((D, tokens), lambda i: (0, 0))]
        out_shape = out_shape + [jax.ShapeDtypeStruct((D, tokens), BF)]
    result = pl.pallas_call(
        functools.partial(attend_kernel, graphs=tokens // LEN, whole=whole, turn=turn, owner=owner),
        grid=(groups,),
        in_specs=[pl.BlockSpec(memory_space=pltpu.SMEM)]
        + [full(x)]
        + ([block(D, PACK)] if whole else [full(a) for a in pieces]),
        out_specs=out_specs,
        out_shape=out_shape,
        compiler_params=pltpu.CompilerParams(vmem_limit_bytes=VMEM_LIMIT),
        cost_estimate=pl.CostEstimate(
            flops=groups * 2_500_000_000, bytes_accessed=groups * 3_000_000, transcendentals=0
        ),
        name="attend",
    )(info, x, *pieces)
    return (pieces[0], result) if whole else (result[0], result[1:])


def attend_back_kernel(xt_ref, qkv_ref, p_ref, aug_ref, go_ref, *refs, graphs):
    *more, g_ref, d_ref = refs
    lane = lanes()
    for g in range(graphs):
        rows = slice(g * LEN, (g + 1) * LEN)
        query, keys, values = qkv_ref[0, 0, rows, :], qkv_ref[0, 1, rows, :], qkv_ref[0, 2, rows, :]
        d_rows, expo = aug_ref[0, rows, :], p_ref[0, rows, :]
        one, zero = jnp.ones_like(values), jnp.zeros_like(values)
        spread = jnp.concatenate(
            [
                jnp.where(
                    head_lanes(h, V_AT), values, jnp.where((lane == h) | (lane == SUB + h), one, zero)
                )
                for h in range(SUB)
            ],
            axis=0,
        )
        d_scores = (expo.astype(F32) * nt(d_rows, spread)).astype(BF)
        d_query = nn(d_scores, by_head(keys, 0)) * SCALE
        d_keys = tn(stack_heads(d_scores), by_head(query, 0)) * SCALE
        d_values = tn(stack_heads(expo), by_head(d_rows, V_AT))
        rolled_keys, rolled_values = pltpu.roll(d_keys, SW, 1), pltpu.roll(d_values, V_AT, 1)
        d_ref[0, rows, 0:128] = jnp.where(lane < SW, d_query, rolled_keys).astype(BF)
        d_ref[0, rows, 128:256] = jnp.where(lane < 64, rolled_keys, rolled_values).astype(BF)
        d_ref[0, rows, 256:384] = jnp.where(lane < V_AT, rolled_values, 0.0).astype(BF)
    grad = nn(xt_ref[...], d_ref[0])
    end = jnp.where(lane < V_AT, grad[:, 256:384], go_ref[0].astype(F32))
    if not more:
        g_ref[0, :, 0:256] = grad[:, 0:256].astype(BF)
        g_ref[0, :, 256:384] = end.astype(BF)
        return
    info_ref, came_ref = more
    outs, size = g_ref.shape[2], g_ref.shape[3]
    for o in range(outs):
        for i in range(2):
            rows = slice((o * 2 + i) * size, (o * 2 + i + 1) * size)
            at = lax.rem(i + info_ref[1], 2)
            came = came_ref[0, rows, :].astype(F32)
            g_ref[0, at, o, :, 0:256] = (grad[rows, 0:256] + came[:, 0:256]).astype(BF)
            g_ref[0, at, o, :, 256:384] = (end[rows] + came[:, 256:384]).astype(BF)


def attend_back(xt, saved, aug, grad_out, first, stride, groups, more=(), outs=0):
    qkv, expo = saved[:2]
    tokens = xt.shape[1]
    shape = (2, outs, D // (2 * outs), PACK) if more else (D, PACK)
    block = lambda *tail: pl.BlockSpec(
        (1,) + tail, lambda i: (first + i * stride,) + (0,) * len(tail)
    )
    out = lambda *tail: pl.BlockSpec((1,) + tail, lambda i: (i,) + (0,) * len(tail))
    return pl.pallas_call(
        functools.partial(attend_back_kernel, graphs=tokens // LEN),
        grid=(groups,),
        in_specs=[
            pl.BlockSpec(xt.shape, lambda i: (0, 0)),
            block(3, tokens, 128),
            block(tokens, 512),
            block(tokens, 128),
            block(D, 128),
        ]
        + ([pl.BlockSpec(memory_space=pltpu.SMEM), block(D, PACK)] if more else []),
        out_specs=[out(*shape), out(tokens, PACK)],
        out_shape=[
            jax.ShapeDtypeStruct((groups,) + shape, BF),
            jax.ShapeDtypeStruct((groups, tokens, PACK), BF),
        ],
        compiler_params=pltpu.CompilerParams(vmem_limit_bytes=VMEM_LIMIT),
        cost_estimate=pl.CostEstimate(
            flops=groups * 4_000_000_000, bytes_accessed=groups * 3_000_000, transcendentals=0
        ),
        name="attend_back",
    )(xt, qkv, expo, aug, grad_out, *more)


def first_sum_kernel(*refs, parts):
    d_refs, w_refs, out_ref = refs[: len(parts)], refs[len(parts) : -1], refs[-1]
    total = jnp.zeros(out_ref.shape, F32)
    for d_ref, (which, picks) in zip(d_refs, parts):
        for j in range(0, len(picks), 2):
            pair = range(j, min(j + 2, len(picks)))
            left = jnp.concatenate([d_ref[k] for k in pair], axis=1)
            right = jnp.concatenate([w_refs[which][picks[k]] for k in pair], axis=1)
            total = total + nt(left, right)
    out_ref[...] = total


def first_sum(ds, parts, weights):
    tokens = ds[0].shape[1]
    rows = LEN * min(2, tokens // LEN)
    full = lambda a: pl.BlockSpec(a.shape, lambda i: (0,) * a.ndim)
    return pl.pallas_call(
        functools.partial(first_sum_kernel, parts=parts),
        grid=(tokens // rows,),
        in_specs=[pl.BlockSpec((d.shape[0], rows, PACK), lambda i: (0, i, 0)) for d in ds]
        + [full(w) for w in weights],
        out_specs=pl.BlockSpec((rows, D), lambda i: (i, 0)),
        out_shape=jax.ShapeDtypeStruct((tokens, D), F32),
        compiler_params=pltpu.CompilerParams(vmem_limit_bytes=VMEM_LIMIT),
        cost_estimate=pl.CostEstimate(
            flops=7_000_000_000, bytes_accessed=12_000_000, transcendentals=0
        ),
        name="first_sum",
    )(*ds, *weights)


def first_back_kernel(
    e_ref, dmid_ref, ident_ref, gain_ref, sum_ref, even_ref, odd_ref, w_ref, out_ref, acc
):
    step, steps = pl.program_id(0), pl.num_programs(0)
    d_normed = sum_ref[...]
    for at, d_ref in enumerate((even_ref, odd_ref)):
        left = jnp.concatenate([d_ref[0], d_ref[1]], axis=1)
        d_normed = d_normed + nt(left, jnp.concatenate([w_ref[at], w_ref[at + 2]], axis=1))
    xhat, rstd = normalize(e_ref[...])
    d_emb = dmid_ref[...] + norm_back(d_normed, xhat, rstd, gain_ref[GAIN : GAIN + 1, :])
    part = tn(ident_ref[...], d_emb.astype(BF))
    part_gain = jnp.sum((d_normed * xhat).reshape(-1, 8, D), axis=0)

    @pl.when(step == 0)
    def _():
        acc[0 : 2 * LAP, :] = part
        acc[2 * LAP :, :] = part_gain

    @pl.when(step > 0)
    def _():
        acc[0 : 2 * LAP, :] += part
        acc[2 * LAP :, :] += part_gain

    @pl.when(step == steps - 1)
    def _():
        out_ref[...] = acc[...]


def first_back(embedded, d_middle, ident_rows, gains, total, d_even, d_odd, weights):
    tokens = embedded.shape[0]
    rows = LEN * min(2, tokens // LEN)
    full = lambda a: pl.BlockSpec(a.shape, lambda i: (0,) * a.ndim)
    tile = pl.BlockSpec((rows, D), lambda i: (i, 0))
    return pl.pallas_call(
        first_back_kernel,
        grid=(tokens // rows,),
        in_specs=[tile, tile, pl.BlockSpec((rows, 2 * LAP), lambda i: (i, 0)), full(gains), tile]
        + [pl.BlockSpec((2, rows, PACK), lambda i: (0, i, 0))] * 2
        + [full(weights)],
        out_specs=pl.BlockSpec((2 * LAP + 8, D), lambda i: (0, 0)),
        out_shape=jax.ShapeDtypeStruct((2 * LAP + 8, D), F32),
        scratch_shapes=[pltpu.VMEM((2 * LAP + 8, D), F32)],
        compiler_params=pltpu.CompilerParams(vmem_limit_bytes=VMEM_LIMIT),
        cost_estimate=pl.CostEstimate(
            flops=4_000_000_000, bytes_accessed=10_000_000, transcendentals=0
        ),
        name="first_back",
    )(embedded, d_middle, ident_rows, gains, total, d_even, d_odd, weights)


def normal_parts(x):
    falling = jnp.exp(-0.5 * x * x)
    t = 1.0 / (1.0 + (0.3275911 * 0.5**0.5) * jnp.abs(x))
    tail = 0.5 * 1.061405429
    for c in (-1.453152027, 1.421413741, -0.284496736, 0.254829592):
        tail = tail * t + 0.5 * c
    tail = tail * t * falling
    return jnp.where(x < 0.0, tail, 1.0 - tail), 0.3989422804014327 * falling


def normalize(values):
    centred = values - jnp.mean(values, axis=-1, keepdims=True)
    spread = jnp.mean(centred * centred, axis=-1, keepdims=True)
    rstd = lax.rsqrt(spread + NORM_EPS)
    return centred * rstd, rstd


def two_parts(v):
    high = v.astype(BF)
    return high, (v - high.astype(F32)).astype(BF)


def forward_kernel(
    info_ref, e_ref, gain_ref, ffn_ref, other_ref, *refs, tile_graphs, waves, groups
):
    o_refs, w_refs = refs[:waves], refs[waves : 2 * waves]
    mid_ref, slope_ref, pay_ref, up_ref, down_ref, hsum, msum = refs[2 * waves :]
    step, steps = pl.program_id(0), pl.num_programs(0)
    core = info_ref[3]

    @pl.when((step == 0) & (core == 0))
    def _():
        up_ref[...] = ffn_ref[...]
        down_ref[...] = other_ref[...]

    @pl.when((step == 0) & (core != 0))
    def _():
        up_ref[...] = other_ref[...]
        down_ref[...] = ffn_ref[...]

    middle = e_ref[...]
    for wave in range(waves):
        left = jnp.concatenate([o_refs[wave][j] for j in range(groups)], axis=1)
        right = jnp.concatenate([w_refs[wave][j][:, 256:] for j in range(groups)], axis=1)
        middle = middle + nt(left, right)
    mid_ref[...] = middle
    xhat, _ = normalize(middle)
    up = nn((xhat * gain_ref[GAIN + 1 : GAIN + 2, :]).astype(BF), up_ref[...])
    cdf, density = normal_parts(up)
    hidden = (up * cdf).astype(BF).astype(F32)
    slope_ref[...] = (cdf + up * density).astype(BF)
    place = lax.broadcasted_iota(jnp.int32, (LEN, 1), 0)
    for j in range(tile_graphs):
        g = step * tile_graphs + j
        live = place < info_ref[LENS + g]
        rows = slice(j * LEN, (j + 1) * LEN)
        hsum[pl.ds(g, 1), :] = jnp.sum(jnp.where(live, hidden[rows], 0.0), axis=0, keepdims=True)
        msum[pl.ds(g, 1), :] = jnp.sum(jnp.where(live, middle[rows], 0.0), axis=0, keepdims=True)

    @pl.when(step == steps - 1)
    def _():
        graphs = hsum.shape[0]
        high, low = two_parts(hsum[...])
        which = lax.broadcasted_iota(jnp.int32, (graphs, 1), 0)
        length, partner = jnp.ones((graphs, 1), F32), jnp.zeros((graphs, 1), F32)
        for g in range(graphs):
            length = jnp.where(which == g, info_ref[LENS + g].astype(F32), length)
            partner = jnp.where(which == g, info_ref[LENS + graphs + g].astype(F32), partner)
        pooled = (msum[...] + (nt(high, down_ref[...]) + nt(low, down_ref[...]))) / length
        xhat_pool, rstd = normalize(pooled)
        high, low = two_parts(xhat_pool)
        pay_ref[:, 0:D] = high
        pay_ref[:, D : 2 * D] = low
        pay_ref[:, 2 * D : 3 * D] = hsum[...].astype(BF)
        lane = lanes()
        stats = jnp.zeros((graphs, 128), F32)
        for at, value in enumerate(two_parts(rstd) + two_parts(1.0 / length) + (partner,)):
            stats = jnp.where(lane == at, value.astype(F32), stats)
        pay_ref[:, 3 * D :] = stats.astype(BF)


def forward_rest(info, embedded, gains, w_up, w_down, outs, weights):
    tokens = embedded.shape[0]
    graphs = tokens // LEN
    tile_graphs = min(2, graphs)
    rows = tile_graphs * LEN
    waves, groups = len(outs), outs[0].shape[0]
    full = lambda a: pl.BlockSpec(a.shape, lambda i: (0,) * a.ndim)
    tile = pl.BlockSpec((rows, D), lambda i: (i, 0))
    return pl.pallas_call(
        functools.partial(forward_kernel, tile_graphs=tile_graphs, waves=waves, groups=groups),
        grid=(tokens // rows,),
        in_specs=[pl.BlockSpec(memory_space=pltpu.SMEM)]
        + [tile, full(gains), full(w_up), full(w_down)]
        + [pl.BlockSpec((groups, rows, 128), lambda i: (0, i, 0)) for _ in outs]
        + [full(w) for w in weights],
        out_specs=[
            tile,
            tile,
            pl.BlockSpec((graphs, 3 * D + 128), lambda i: (0, 0)),
            full(w_up),
            full(w_down),
        ],
        out_shape=[
            jax.ShapeDtypeStruct((tokens, D), F32),
            jax.ShapeDtypeStruct((tokens, D), BF),
            jax.ShapeDtypeStruct((graphs, 3 * D + 128), BF),
            jax.ShapeDtypeStruct(w_up.shape, BF),
            jax.ShapeDtypeStruct(w_down.shape, BF),
        ],
        scratch_shapes=[pltpu.VMEM((graphs, D), F32), pltpu.VMEM((graphs, D), F32)],
        compiler_params=pltpu.CompilerParams(vmem_limit_bytes=VMEM_LIMIT),
        cost_estimate=pl.CostEstimate(
            flops=10_000_000_000, bytes_accessed=20_000_000, transcendentals=0
        ),
        name="forward_rest",
    )(info, embedded, gains, w_up, w_down, *outs, *weights)


def norm_back(d_normed, xhat, rstd, gain):
    d_hat = d_normed * gain
    return rstd * (
        d_hat
        - jnp.mean(d_hat, axis=-1, keepdims=True)
        - xhat * jnp.mean(d_hat * xhat, axis=-1, keepdims=True)
    )


def ffn_back_kernel(
    info_ref, mid_ref, slope_ref, dout_ref, dhid_ref, gain_ref, up_ref, *refs, tile_graphs, groups
):
    o_refs, rinv_refs, w_refs = refs[0:2], refs[2:4], refs[4:6]
    dmid_ref, grad_ref, dgain_ref = refs[6:9]
    aug_refs, go_refs = refs[9:11], refs[11:13]
    grad, dgain, grad_out = refs[13:]
    step, steps = pl.program_id(0), pl.num_programs(0)
    xhat, rstd = normalize(mid_ref[...])
    gain = gain_ref[GAIN + 1 : GAIN + 2, :]
    place = lax.broadcasted_iota(jnp.int32, (LEN, 1), 0)
    d_up, d_out = [], []
    for j in range(tile_graphs):
        g = step * tile_graphs + j
        live = place < info_ref[LENS + g]
        rows = slice(j * LEN, (j + 1) * LEN)
        d_hidden = jnp.where(live, dhid_ref[pl.ds(g, 1), :], 0.0)
        d_up.append((slope_ref[rows, :].astype(F32) * d_hidden).astype(BF))
        d_out.append(jnp.where(live, dout_ref[pl.ds(g, 1), :], 0.0))
    d_up, d_out = jnp.concatenate(d_up, axis=0), jnp.concatenate(d_out, axis=0)
    d_normed = nt(d_up, up_ref[...])
    d_mid = d_out + norm_back(d_normed, xhat, rstd, gain)
    dmid_ref[...] = d_mid
    d_attn = d_mid.astype(BF)
    d_turned = d_attn.T
    part = tn((xhat * gain).astype(BF), d_up)
    part_gain = jnp.sum((d_normed * xhat).reshape(-1, 8, D), axis=0)

    lane = lanes()
    row = lax.broadcasted_iota(jnp.int32, (256, 128), 0) & 127
    column = lax.broadcasted_iota(jnp.int32, (256, 128), 1)
    pick = jnp.zeros((256, 128), BF)
    for h in range(SUB):
        inside = (row >= V_AT + h * HEAD_DIM) & (row < V_AT + (h + 1) * HEAD_DIM)
        pick = jnp.where(inside & ((column == h) | (column == SUB + h)), jnp.ones_like(pick), pick)
    parts_out = []
    for half in range(2):
        d_heads = nn(d_attn, jnp.concatenate([w_refs[half][j] for j in range(groups)], axis=1))
        for j in range(groups):
            d_over = d_heads[:, j * 128 : (j + 1) * 128] * rinv_refs[half][j]
            d_over = jnp.where(lane >= V_AT, d_over, 0.0)
            terms = d_over * o_refs[half][j].astype(F32)
            delta = nn(jnp.concatenate(two_parts(terms), axis=1), pick)
            rounded = delta.astype(BF).astype(F32)
            aug_refs[half][j] = jnp.where(
                lane >= V_AT, d_over, jnp.where(lane < SUB, -rounded, rounded - delta)
            ).astype(BF)
        parts_out.append(
            nn(d_turned, jnp.concatenate([o_refs[half][j] for j in range(groups)], axis=1))
        )

    @pl.when(step == 0)
    def _():
        grad[...] = part
        dgain[...] = part_gain
        for half in range(2):
            grad_out[half] = parts_out[half]

    @pl.when(step > 0)
    def _():
        grad[...] += part
        dgain[...] += part_gain
        for half in range(2):
            grad_out[half] += parts_out[half]

    @pl.when(step == steps - 1)
    def _():
        for half in range(2):
            grad_ref[half] = grad[:, half * PACK : (half + 1) * PACK].astype(BF)
            for j in range(groups):
                go_refs[half][j] = grad_out[half, :, j * 128 : (j + 1) * 128].astype(BF)
        dgain_ref[...] = dgain[...]


def ffn_back(info, middle, slope, d_out, d_hidden, gains, w_up, outs, rinvs, weights):
    tokens = middle.shape[0]
    tile_graphs = min(2, tokens // LEN)
    rows = tile_graphs * LEN
    groups = outs[0].shape[0]
    full = lambda a: pl.BlockSpec(a.shape, lambda i: (0,) * a.ndim)
    tile = pl.BlockSpec((rows, D), lambda i: (i, 0))
    sub_tile = pl.BlockSpec((groups, rows, 128), lambda i: (0, i, 0))
    result = pl.pallas_call(
        functools.partial(ffn_back_kernel, tile_graphs=tile_graphs, groups=groups),
        grid=(tokens // rows,),
        in_specs=[pl.BlockSpec(memory_space=pltpu.SMEM), tile, tile]
        + [full(a) for a in (d_out, d_hidden, gains, w_up)]
        + [sub_tile] * 4
        + [pl.BlockSpec((groups, D, 128), lambda i: (0, 0, 2))] * 2,
        out_specs=[
            tile,
            pl.BlockSpec((2, D, PACK), lambda i: (0, 0, 0)),
            pl.BlockSpec((8, D), lambda i: (0, 0)),
        ]
        + [sub_tile] * 2
        + [pl.BlockSpec((groups, D, 128), lambda i: (0, 0, 0))] * 2,
        out_shape=[
            jax.ShapeDtypeStruct((tokens, D), F32),
            jax.ShapeDtypeStruct((2, D, PACK), BF),
            jax.ShapeDtypeStruct((8, D), F32),
        ]
        + [jax.ShapeDtypeStruct((groups, tokens, 128), BF)] * 2
        + [jax.ShapeDtypeStruct((groups, D, 128), BF)] * 2,
        scratch_shapes=[
            pltpu.VMEM((D, D), F32),
            pltpu.VMEM((8, D), F32),
            pltpu.VMEM((2, D, groups * 128), F32),
        ],
        compiler_params=pltpu.CompilerParams(vmem_limit_bytes=VMEM_LIMIT),
        cost_estimate=pl.CostEstimate(
            flops=14_000_000_000, bytes_accessed=20_000_000, transcendentals=0
        ),
        name="ffn_back",
    )(info, middle, slope, d_out, d_hidden, gains, w_up, *outs, *rinvs, *weights)
    return result[:3], result[3:5], result[5:7]


def loss_kernel(
    info_ref, a1_ref, a3_ref, b1_ref, b3_ref, gain_ref, down_ref,
    loss_ref, dout_ref, dhid_ref, dlow_ref, hid_ref, dgain_ref, xhat, stats, rows_ref
):
    outs, graphs = a1_ref.shape[1], a1_ref.shape[2]
    outer, inner, far, core = (info_ref[i] for i in range(4))
    count = outs * 2 * GRAPHS_DEV
    place = lambda f, o, i, c: pl.multiple_of(
        f * count + (o * 2 + i) * GRAPHS_DEV + c * graphs, graphs
    )
    for owner, refs in ((core, (a1_ref, a3_ref)), (1 - core, (b1_ref, b3_ref))):
        for part, ref in enumerate(refs):
            for at in range(2):
                if part == at:
                    f, i = part, part
                else:
                    f, i = (owner, 1 - owner) if part == 0 else (1 - owner, owner)
                for o in range(outs):
                    values = ref[at, o].astype(F32)
                    row = place(
                        lax.rem(far + f, 2), lax.rem(outer + outs - o, outs), lax.rem(inner + i, 2), owner
                    )
                    rows = pl.ds(row, graphs)
                    xhat[rows, :] = values[:, 0:D] + values[:, D : 2 * D]
                    rows_ref[rows, :] = values[:, 2 * D : 3 * D]
                    stats[rows, :] = values[:, 3 * D :]
    hid_ref[...] = rows_ref[...].astype(BF)
    root = D**-0.5
    left, right = xhat[0:count, :] * gain_ref[GAIN + 2 : GAIN + 3, :], xhat[count:, :] * gain_ref[GAIN + 2 : GAIN + 3, :]
    exact = lambda a, b, dims: lax.dot_general(
        a, b, (dims, ((), ())), precision=HIGHEST, preferred_element_type=F32
    )
    logits = exact(left, right, ((1,), (1,))) * root
    row_top, col_top = jnp.max(logits, axis=1, keepdims=True), jnp.max(logits, axis=0, keepdims=True)
    row_expo, col_expo = jnp.exp(logits - row_top), jnp.exp(logits - col_top)
    row_sum, col_sum = jnp.sum(row_expo, axis=1, keepdims=True), jnp.sum(col_expo, axis=0, keepdims=True)
    row_id = lax.broadcasted_iota(jnp.int32, (count, count), 0)
    col_id = lax.broadcasted_iota(jnp.int32, (count, count), 1)
    slot = stats[0:count, 4:5].astype(jnp.int32)
    positive = jnp.where(col_id == (row_id & -GRAPHS_DEV) + slot, 1.0, 0.0)
    loss = (
        jnp.sum(row_top + jnp.log(row_sum), axis=0, keepdims=True)
        + jnp.sum(col_top + jnp.log(col_sum), axis=1, keepdims=True)
        - 2.0 * jnp.sum(jnp.sum(positive * logits, axis=1, keepdims=True), axis=0, keepdims=True)
    )
    loss_ref[...] = loss
    d_logits = row_expo / row_sum + col_expo / col_sum - 2.0 * positive
    rows_ref[0:count, :] = exact(d_logits, right, ((1,), (0,))) * root
    rows_ref[count:, :] = exact(d_logits, left, ((0,), (0,))) * root
    every = xhat[...]
    d_summary = rows_ref[...]
    dgain_ref[...] = jnp.sum(d_summary * every, axis=0, keepdims=True)
    rstd, share = stats[:, 0:1] + stats[:, 1:2], stats[:, 2:3] + stats[:, 3:4]
    d_rows = norm_back(d_summary, every, rstd, gain_ref[GAIN + 2 : GAIN + 3, :]) * share
    rows_ref[...] = d_rows
    dlow_ref[...] = d_rows.astype(BF)
    own = rows_ref[pl.ds(place(far, outer, inner, core), graphs), :]
    dout_ref[...] = own
    dhid_ref[...] = nn(own.astype(BF), down_ref[...])


def contrast(info, pieces, gains, w_down):
    outs, graphs = pieces[0].shape[1], pieces[0].shape[2]
    total = outs * 4 * GRAPHS_DEV
    return pl.pallas_call(
        loss_kernel,
        in_specs=[pl.BlockSpec(memory_space=pltpu.SMEM)]
        + [pl.BlockSpec(memory_space=pltpu.VMEM)] * 6,
        out_specs=[pl.BlockSpec(memory_space=pltpu.VMEM)] * 6,
        out_shape=[
            jax.ShapeDtypeStruct((1, 1), F32),
            jax.ShapeDtypeStruct((graphs, D), F32),
            jax.ShapeDtypeStruct((graphs, D), F32),
            jax.ShapeDtypeStruct((total, D), BF),
            jax.ShapeDtypeStruct((total, D), BF),
            jax.ShapeDtypeStruct((1, D), F32),
        ],
        scratch_shapes=[
            pltpu.VMEM((total, D), F32),
            pltpu.VMEM((total, 128), F32),
            pltpu.VMEM((total, D), F32),
        ],
        compiler_params=pltpu.CompilerParams(vmem_limit_bytes=24 * 2**20),
        cost_estimate=pl.CostEstimate(
            flops=3_000_000_000, bytes_accessed=4_000_000, transcendentals=0
        ),
        name="contrast",
    )(info, *pieces, gains, w_down)


def contrast_plain(everyone, gains, w_down, own_row, graphs):
    n = everyone.shape[0]
    stats = everyone[..., 3 * D :].astype(F32)
    xhat = everyone[..., :D].astype(F32) + everyone[..., D : 2 * D].astype(F32)
    hidden_sums = everyone[..., 2 * D : 3 * D].reshape(-1, D)
    rstd_pool = (stats[..., 0:1] + stats[..., 1:2]).reshape(-1, 1)
    share = (stats[..., 2:3] + stats[..., 3:4]).reshape(-1, 1)
    summaries = xhat * gains[GAIN + 2]
    left, right = summaries[:, 0].reshape(-1, D), summaries[:, 1].reshape(-1, D)
    root_width = D**0.5
    logits = jnp.dot(left, right.T, precision=HIGHEST) / root_width
    row_totals, col_totals = log_total(logits, 1), log_total(logits, 0)
    count = logits.shape[0]
    group = jnp.arange(count, dtype=jnp.int32) // GRAPHS_DEV
    partners = group * GRAPHS_DEV + stats[:, 0, :, 4].reshape(-1).astype(jnp.int32)
    positive = (partners[:, None] == jnp.arange(count, dtype=jnp.int32)[None, :]).astype(F32)
    total_loss = jnp.sum(row_totals) + jnp.sum(col_totals) - 2.0 * jnp.sum(positive * logits)
    d_logits = (
        jnp.exp(logits - row_totals[:, None])
        + jnp.exp(logits - col_totals[None, :])
        - 2.0 * positive
    )
    d_left = jnp.dot(d_logits, right, precision=HIGHEST) / root_width
    d_right = jnp.dot(d_logits.T, left, precision=HIGHEST) / root_width
    d_summary = jnp.stack(
        [d_left.reshape(n, GRAPHS_DEV, D), d_right.reshape(n, GRAPHS_DEV, D)], axis=1
    ).reshape(-1, D)
    xhat = xhat.reshape(-1, D)
    gain_three = jnp.sum(d_summary * xhat, axis=0, keepdims=True)
    d_rows = norm_back(d_summary, xhat, rstd_pool, gains[GAIN + 2]) * share
    d_out = lax.dynamic_slice_in_dim(d_rows, own_row, graphs, 0)
    d_hidden = nn(d_out.astype(BF), w_down)
    return total_loss, d_out, d_hidden, d_rows.astype(BF), hidden_sums, gain_three


class Place:
    def __init__(self):
        self.n, self.heads = lax.axis_size("dp"), lax.axis_size("head")
        self.outs = self.n // 2
        dp, head = lax.axis_index("dp"), lax.axis_index("head")
        self.dp, self.head = dp, head
        self.outer, self.inner, self.far, self.core = dp // 2, dp % 2, head // 2, head % 2

    def move(self, v, to):
        pairs = []
        for i in range(self.n * self.heads):
            outer, inner, far, core = i // 8, (i // 4) % 2, (i // 2) % 2, i % 2
            outer, inner, far, core = to(outer, inner, far, core)
            pairs.append((i, ((outer % self.outs * 2 + inner) * 2 + far) * 2 + core))
        return lax.ppermute(v, ("dp", "head"), pairs)

    def to_core(self, v):
        return self.move(v, lambda o, i, f, c: (o, i, f, 1 - c))

    def to_outer(self, v, by):
        return self.move(v, lambda o, i, f, c: (o + by, i, f, c))

    def mixed(self, v, turn):
        return self.move(
            v, lambda o, i, f, c: (o, 1 - i, f, c) if c == turn else (o, i, 1 - f, c)
        )

    def by_core(self, a, b):
        return jnp.where(self.core == 0, a, b)

    def gather_outer(self, v):
        out = jnp.zeros((self.outs,) + v.shape, v.dtype)
        out = lax.dynamic_update_index_in_dim(out, v, self.outer, 0)
        for by in range(1, self.outs):
            out = lax.dynamic_update_index_in_dim(
                out, self.to_outer(v, by), (self.outer - by) % self.outs, 0
            )
        return out

    def outer_list(self, v):
        return jnp.stack([v] + [self.to_outer(v, by) for by in range(1, self.outs)])

    def gather_pieces(self, v):
        return self.gather_near(self.gather_outer(v))

    def gather_near(self, own):
        return self.gather_last(own, self.mixed(own, 0))

    def gather_last(self, own, second):
        return self.pieces_of(own, second, self.mixed(jnp.stack([own, second]), 1))

    def pieces_of(self, own, second, third):
        return [
            [own, self.by_core(second, third[0])],
            [self.by_core(third[0], second), third[1]],
        ]

    def whole(self, pieces):
        rows = [
            [jnp.where(self.far == 0, pieces[f][i], pieces[1 - f][i]) for f in range(2)]
            for i in range(2)
        ]
        ordered = [
            [jnp.where(self.inner == 0, rows[i][f], rows[1 - i][f]) for f in range(2)]
            for i in range(2)
        ]
        return jnp.stack([jnp.stack(pair, axis=1) for pair in ordered], axis=1)

    def both_cores(self, v, axis):
        other = self.to_core(v)
        return jnp.stack([self.by_core(v, other), self.by_core(other, v)], axis=axis)

    def both_cores_of(self, own, sent):
        other = self.to_core(sent)
        return jnp.stack([self.by_core(own, other), self.by_core(other, own)])

    def gather_all(self, v):
        v = self.both_cores(self.whole(self.gather_pieces(v)), 3)
        return v.reshape((self.n, self.heads) + v.shape[4:])

    def fold_far(self, pieces):
        sent = jnp.stack([self.by_core(pieces[1][0], pieces[0][1]), pieces[1][1]])
        kept = jnp.stack([pieces[0][0], self.by_core(pieces[0][1], pieces[1][0])])
        return kept, sent

    def fold_near(self, kept, came, dtype):
        total = kept.astype(F32) + came.astype(F32)
        return total[0], total[1].astype(dtype)

    def fold_outer(self, kept, came, dtype):
        total = (kept.astype(F32) + came.astype(F32)).astype(dtype)
        pick = lambda by: lax.dynamic_index_in_dim(
            total, (self.outer + by) % self.outs, 0, keepdims=False
        )
        result = pick(0).astype(F32)
        for by in range(1, self.outs):
            result = result + self.to_outer(pick(by), by).astype(F32)
        return result

    def total(self, v):
        v = jnp.broadcast_to(v, (self.n * self.heads, 128))
        return jnp.sum(lax.all_to_all(v, ("dp", "head"), 0, 0, tiled=True)[:, 0])

    def split_rows(self, v):
        v = v.reshape((self.outs, 2, -1) + v.shape[1:])
        return [
            lax.dynamic_index_in_dim(v, (self.inner + i) % 2, 1, keepdims=False) for i in range(2)
        ]


def tie(*values):
    return lax.optimization_barrier(values)


def after(value, *others):
    return lax.optimization_barrier((value,) + others)[0]


def log_total(values, axis):
    top = jnp.max(values, axis=axis, keepdims=True)
    return jnp.squeeze(top, axis) + jnp.log(jnp.sum(jnp.exp(values - top), axis=axis))


def identifiers(table, endpoints):
    graphs = endpoints.shape[0] // LEN
    nodes = table.reshape(graphs, NODE, LAP).astype(BF)
    picks = (
        endpoints.reshape(graphs, LEN, 2)[..., None] == jnp.arange(NODE, dtype=jnp.int32)
    ).astype(BF)
    found = jnp.einsum("glan,gnc->glac", picks, nodes, preferred_element_type=F32)
    return found.reshape(graphs * LEN, 2 * LAP).astype(BF)


def stack_pieces(place, near, last):
    pieces = place.pieces_of(near[0], near[1], last)
    packs = []
    for f in range(2):
        for c in range(2):
            rows = [
                jnp.where(place.inner == i, pieces[f][0][:, c], pieces[f][1][:, c]) for i in range(2)
            ]
            packs.append(jnp.stack(rows, axis=1).reshape(D, PACK))
    return jnp.stack(packs)


def split_core(place, grad_up):
    v = grad_up.reshape((2, place.outs, 2, 2, 2, -1, PACK))
    pick = lambda at: lax.dynamic_index_in_dim(v, at, 4, keepdims=False)
    return pick(1 - place.core), pick(place.core)


def fold_pieces(place, own, came, up):
    pieces = []
    for f in range(2):
        total = own[f].astype(F32) + came[f].astype(F32)
        pieces.append([v.astype(BF) for v in place.split_rows(total)])
    if up is None:
        return pieces
    total = (up[0].astype(F32) + up[1].astype(F32)).astype(BF)
    for f in range(2):
        part = lax.dynamic_index_in_dim(total, (place.far + f) % 2, 3, keepdims=False)
        for i in range(2):
            rows = lax.dynamic_index_in_dim(part, (place.inner + i) % 2, 2, keepdims=False)
            pieces[f][i] = jnp.concatenate([pieces[f][i], rows[0], rows[1]], axis=1)
    return pieces


def squares_kernel(*refs):
    *grad_refs, out_ref = refs
    total = jnp.zeros((1, 1), F32)
    for ref in grad_refs:
        v = ref[...]
        total = total + jnp.sum(jnp.sum(v * v, axis=0, keepdims=True), axis=1, keepdims=True)
    out_ref[...] = jnp.broadcast_to(total, out_ref.shape)


def squares(grads, devices):
    return pl.pallas_call(
        squares_kernel,
        out_shape=jax.ShapeDtypeStruct((devices, 128), F32),
        cost_estimate=pl.CostEstimate(flops=1_000_000, bytes_accessed=500_000, transcendentals=0),
        name="squares",
    )(*grads)


def update_kernel(parts_ref, *refs):
    count = len(STEP_RATES)
    grads, weights, firsts, seconds = (refs[k * count : (k + 1) * count] for k in range(4))
    norm_ref, refs = refs[4 * count], refs[4 * count + 1 :]
    new_weights, new_firsts, new_seconds = (refs[k * count : (k + 1) * count] for k in range(3))
    norm = jnp.sqrt(jnp.sum(parts_ref[...], axis=0, keepdims=True)[:, 0:1])
    norm_ref[...] = norm
    factor = CLIP_AT / jnp.maximum(norm, CLIP_AT)
    for k, rate in enumerate(STEP_RATES):
        for at in range(grads[k].shape[0]) if len(grads[k].shape) == 3 else (...,):
            weight = weights[k][at]
            clipped = grads[k][at] * factor
            first = BETA_ONE * firsts[k][at] + (1.0 - BETA_ONE) * clipped
            second = BETA_TWO * seconds[k][at] + (1.0 - BETA_TWO) * clipped * clipped
            first_hat = first / (1.0 - BETA_ONE**STEPS)
            second_hat = second / (1.0 - BETA_TWO**STEPS)
            new_weights[k][at] = weight - rate * (
                first_hat / (jnp.sqrt(second_hat) + ADAM_EPS) + DECAY * weight
            )
            new_firsts[k][at] = first
            new_seconds[k][at] = second


def update(norm_parts, grads, state):
    result = pl.pallas_call(
        update_kernel,
        out_shape=[jax.ShapeDtypeStruct((1, 1), F32)]
        + [jax.ShapeDtypeStruct(v.shape, F32) for kind in state for v in kind],
        cost_estimate=pl.CostEstimate(
            flops=5_000_000, bytes_accessed=6_000_000, transcendentals=0
        ),
        name="update",
    )(norm_parts, *grads, *(v for kind in state for v in kind))
    count = len(grads)
    return result[0], [result[1 + k * count : 1 + (k + 1) * count] for k in range(3)]


def per_device(
    features,
    laplacian,
    endpoints,
    lengths,
    pairing,
    ident_weight,
    qkv_weight,
    out_weight,
    ffn_weight,
    norm_gains,
    ident_first,
    qkv_first,
    out_first,
    ffn_first,
    gains_first,
    ident_second,
    qkv_second,
    out_second,
    ffn_second,
    gains_second,
):
    place = Place()
    heads, head, dp, core = place.heads, place.head, place.dp, place.core
    tokens = features.shape[0] // heads
    graphs = tokens // LEN
    own_columns = norm_gains.shape[1]

    small = jnp.concatenate([ident_weight, norm_gains], axis=0)
    small_rows = small.shape[0]

    packed = [qkv_weight[:, 0], qkv_weight[:, 1], qkv_weight[:, 2], out_weight.T]
    shards = jnp.stack(
        [
            jnp.concatenate([m[:, s * SW : (s + 1) * SW] for m in packed], axis=1).astype(BF)
            for s in range(2)
        ]
    )
    pick = lambda v, at: lax.dynamic_index_in_dim(v, at, 0, keepdims=False)
    near = jnp.stack([pick(shards, core), place.to_core(pick(shards, 1 - core))])
    shard_rows = D // place.n
    aligned = shard_rows % 16 == 0
    devices = place.n * heads
    small = jnp.broadcast_to(after(small.reshape(1, -1), near), (devices, small.size))
    small = lax.all_to_all(small, ("dp", "head"), 0, 0, tiled=True)
    near_own = (place.outer_list if aligned else place.gather_outer)(near)
    ffn = after(ffn_weight.astype(BF), near_own)
    ffn_near = place.both_cores_of(pick(ffn, core), pick(ffn, 1 - core))
    ffn_own = place.gather_outer(ffn_near)
    near_own = after(near_own, small)
    near = jnp.stack([near_own, place.mixed(near_own, 0)])
    last = place.mixed(near, 1)
    near_others = place.to_core(near)
    ffn_own = after(ffn_own, near)
    ffn_next = place.mixed(ffn_own, 0)
    ffn_last = place.mixed(jnp.stack([ffn_own, ffn_next]), 1)
    small = small.reshape(-1, small_rows, own_columns).transpose(1, 0, 2).reshape(small_rows, D)
    ident_full, gains = after(small[: 2 * LAP].astype(BF), near), small
    start_row = head * tokens
    lens = lax.dynamic_slice_in_dim(lengths.reshape(-1), head * graphs, graphs, 0)
    partner = lax.dynamic_slice_in_dim(
        jnp.concatenate([pairing.reshape(-1)] * 2), head * graphs, graphs, 0
    )
    places = jnp.stack([place.outer, place.inner, place.far, core, 1 - core]).astype(jnp.int32)
    info = jnp.concatenate([places, lens, partner])
    table_rows = lax.dynamic_slice_in_dim(laplacian, head * graphs * NODE, graphs * NODE, 0)
    end_rows = lax.dynamic_slice_in_dim(endpoints, start_row, tokens, 0)
    ident_rows = identifiers(table_rows, end_rows)
    embedded = lax.dynamic_slice_in_dim(features, start_row, tokens, 0).astype(F32)
    embedded = embedded + nn(ident_rows, ident_full)
    normed_one = (normalize(embedded)[0] * gains[GAIN]).astype(BF)

    last_others = place.to_core(last)
    if aligned:
        mine, saved_mine = attend(info, 3, normed_one, [near, last], True)
    else:
        packs = stack_pieces(place, near, last)
        mine, saved_mine = attend(info, 3, normed_one, [packs], True)
    normed_turned = saved_mine[4]
    heads_mine = saved_mine[2]
    ffn_pieces = place.pieces_of(ffn_own, ffn_next, after(ffn_last, heads_mine))
    if aligned:
        others, saved_others = attend(info, 4, normed_one, [near_others, last_others], False)
    else:
        others, saved_others = attend(info, 4, normed_one, [place.to_core(packs)], False)
    ffn_mine = place.whole(ffn_pieces).reshape(D, -1)
    ffn_other = place.to_core(ffn_mine)
    middle, slope, payload, w_up, w_down = forward_rest(
        info,
        embedded,
        gains,
        ffn_mine,
        ffn_other,
        [heads_mine, saved_others[2]],
        [mine, others],
    )

    own_row = (dp * heads + head) * graphs
    if place.n * GRAPHS_DEV <= 128:
        first = place.outer_list(payload)
        first = jnp.stack([first, place.mixed(first, 0)])
        third = place.mixed(first, 1)
        total_loss, d_out, d_hidden, d_rows_low, hidden_sums, gain_three = contrast(
            info, [first, third, place.to_core(first), place.to_core(third)], gains, w_down
        )
        total_loss = total_loss[0, 0]
    else:
        everyone = place.gather_all(payload).reshape(place.n, 2, GRAPHS_DEV, -1)
        total_loss, d_out, d_hidden, d_rows_low, hidden_sums, gain_three = contrast_plain(
            everyone, gains, w_down, own_row, graphs
        )

    own_column = (dp * heads + head) * own_columns
    d_columns = lax.dynamic_slice_in_dim(d_rows_low, own_column, own_columns, 1)
    grad_down = tn(d_columns, hidden_sums)
    (d_middle, grad_up, gain_two), augs, grad_outs = ffn_back(
        info,
        middle,
        slope,
        d_out,
        d_hidden,
        gains,
        w_up,
        [saved_mine[2], saved_others[2]],
        [saved_mine[3], saved_others[3]],
        [mine, others],
    )
    up_sent, up_kept = split_core(place, grad_up)
    up_came = place.to_core(up_sent)
    grad_others, d_others = attend_back(
        normed_turned, saved_others, augs[1], grad_outs[1], 0, 1, heads
    )
    came = place.to_core(grad_others)
    back = functools.partial(attend_back, normed_turned, saved_mine)
    aug = after(augs[0], grad_others)
    grad_even, d_even = back(aug, grad_outs[0], 0, 2, heads // 2)
    even = fold_pieces(place, [grad_even[0], grad_even[1]], [came[0], came[2]], (up_kept, up_came))
    even_kept, even_sent = place.fold_far(even)
    even_came = place.mixed(even_sent, 1)
    more = ([info, came], place.outs) if aligned else ()
    grad_odd, d_odd = back(after(aug, even_sent), grad_outs[0], 1, 2, heads // 2, *more)
    even_kept, even_sent = place.fold_near(even_kept, after(even_came, grad_odd), BF)
    if aligned:
        odd = [[v[0], v[1]] for v in grad_odd]
    else:
        odd = fold_pieces(place, [grad_odd[0], grad_odd[1]], [came[1], came[3]], None)
    odd_kept, odd_sent = place.fold_far(odd)
    odd_came = place.mixed(odd_sent, 1)
    even_came = place.mixed(even_sent, 0)
    d_normed = first_sum([after(d_others, odd_sent)], ((0, (0, 1, 2, 3)),), [others])
    odd_kept, odd_sent = place.fold_near(odd_kept, odd_came, BF)
    odd_sent = after(odd_sent, even_came)
    odd_came = place.mixed(odd_sent, 0)
    even = place.fold_outer(even_kept, even_came, BF)
    rows = first_back(
        embedded, d_middle, ident_rows, gains, d_normed, d_even, after(d_odd, odd_sent), mine
    )
    rows = after(rows, even, odd_came)
    odd = place.fold_outer(odd_kept, odd_came, BF)
    gain_rows = jnp.stack([jnp.sum(rows[2 * LAP :], axis=0), jnp.sum(gain_two, axis=0)])
    rows = jnp.concatenate([rows[: 2 * LAP], gain_rows], axis=0)
    row_count = rows.shape[0]
    rows = rows.T.reshape(devices, own_columns * row_count)
    rows = jnp.sum(lax.all_to_all(rows, ("dp", "head"), 0, 0, tiled=True), axis=0)
    rows = rows.reshape(own_columns, row_count)
    own_gains = lax.dynamic_slice_in_dim(gain_three, own_column, own_columns, 1)
    norm_parts = lax.all_to_all(
        squares([even, odd, grad_down, rows, own_gains], devices),
        ("dp", "head"),
        0,
        0,
        tiled=True,
    )
    own_half, other_half = even[:shard_rows], place.to_core(odd)
    halves = [place.by_core(own_half, other_half), place.by_core(other_half, own_half)]
    columns = lambda j: jnp.concatenate([v[:, j * SW : (j + 1) * SW] for v in halves], axis=1)
    grad_up = even[shard_rows:].reshape(2, own_columns, PACK)
    grads = (
        rows[:, : 2 * LAP],
        jnp.stack([columns(0), columns(1), columns(2)]),
        columns(3).T,
        jnp.stack([jnp.concatenate([grad_up[0], grad_up[1]], axis=1), grad_down]),
        jnp.concatenate([rows[:, 2 * LAP :].T, own_gains], axis=0),
    )
    turns = (lambda v: v.T, lambda v: v.transpose(1, 0, 2)) + (lambda v: v,) * 3
    state = [
        [turn(v) for turn, v in zip(turns, kind)]
        for kind in (
            (ident_weight, qkv_weight, out_weight, ffn_weight, norm_gains),
            (ident_first, qkv_first, out_first, ffn_first, gains_first),
            (ident_second, qkv_second, out_second, ffn_second, gains_second),
        )
    ]
    grad_norm, results = update(norm_parts, grads, state)
    return (grad_norm[0, 0], total_loss) + tuple(
        turn(v) for kind in results for turn, v in zip(turns, kind)
    )


def solution(mesh):
    both = P(None, ("dp", "head"))
    weights = (both, P("dp", None, "head"), P("head", "dp"), P(None, ("dp", "head"), None), both)
    in_specs = (P("dp", None),) * 5 + weights * 3
    out_specs = (P(), P()) + weights * 3
    return jax.shard_map(
        per_device, mesh=mesh, in_specs=in_specs, out_specs=out_specs, check_vma=False
    )
```

profile of v0, /device:TPU:0, one launch (start us, length us, event | category | flops | bytes accessed | tf_op | source)
XLA Modules:
  0.0 260.9 jit_solution(4064150289496427025)
XLA Ops:
  4.6 3.0 %collective-permute-start.1 = (bf16[2,96,384]{2,1,0:T(8,128)(2,1)S(1)}, bf16[2,96,384]{2,1,0:T(8,128)(2,1)S(1)}, u32[]{:S(2)}, u32[]{:S(2)}) collective-permute-start(bf16[2,96,384]{2,1,0:T(8,128)(2,1)S(1)} %get-tuple-element.194), channel_id=1, source_target_pairs={{0,8},{1,9},{2,10},{3,11},{4,12},{5,13},{6,14},{7,15},{8,16},{9,17... | collective-permute-start | bytes 442376 | tf_op jit(solution)/shard_map/ppermute | solution.py:701
  7.6 2.6 collective-permute-start.2
  14.4 5.8 %collective-permute-done.2 = bf16[2,96,384]{2,1,0:T(8,128)(2,1)S(1)} collective-permute-done((bf16[2,96,384]{2,1,0:T(8,128)(2,1)S(1)}, bf16[2,96,384]{2,1,0:T(8,128)(2,1)S(1)}, u32[]{:S(2)}, u32[]{:S(2)}) %collective-permute-start.2) | collective-permute-done | bytes 147488 | tf_op jit(solution)/shard_map/ppermute | solution.py:701
  21.8 7.0 %all-to-all-start = ((f32[32,1,840]{2,1,0:T(1,128)}), f32[32,1,840]{2,1,0:T(1,128)S(1)}, u32[]{:S(2)}, u32[]{:S(2)}) async-start(f32[32,1,840]{2,1,0:T(1,128)} %broadcast_in_dim.24), calls=%async_computation | async-start | bytes 229376 | tf_op jit(solution)/shard_map/all_to_all | solution.py:953
  49.7 3.1 %collective-permute-done.10 = bf16[4,2,24,768]{3,2,1,0:T(8,128)(2,1)S(1)} collective-permute-done((bf16[4,2,24,768]{3,2,1,0:T(8,128)(2,1)S(1)}, bf16[4,2,24,768]{3,2,1,0:T(8,128)(2,1)S(1)}, u32[]{:S(2)}, u32[]{:S(2)}) %collective-permute-start.10) | collective-permute-done | bytes 294944 | tf_op jit(solution)/shard_map/ppermute | solution.py:701
  53.6 7.6 %collective-permute-done.5.refs_1_ = bf16[2,4,2,96,384]{4,3,2,1,0:T(8,128)(2,1)} collective-permute-done((bf16[2,4,2,96,384]{4,3,2,1,0:T(8,128)(2,1)}, bf16[2,4,2,96,384]{4,3,2,1,0:T(8,128)(2,1)}, u32[]{:S(2)}, u32[]{:S(2)}) %collective-permute-start.5) | collective-permute-done | bytes 1179680 | tf_op jit(solution)/shard_map/ppermute | solution.py:701
  61.2 12.9 %attend.2 = (bf16[4,768,384]{2,1,0:T(8,128)(2,1)}, bf16[4,3,1024,128]{3,2,1,0:T(8,128)(2,1)}, bf16[4,1024,512]{2,1,0:T(8,128)(2,1)}, bf16[4,1024,128]{2,1,0:T(8,...) custom-call(s32[21]{0:T(128)S(1)} %concatenate.121.info_ref.refs_0_, ...), custom_call_target="tpu_custom_call" | custom-call | flops 10000000000 | bytes 12000000 | tf_op jit(solution)/shard_map/attend/pallas_call | solution.py:145
  76.5 12.0 %attend.3 = (bf16[4,768,384]{2,1,0:T(8,128)(2,1)}, bf16[4,3,1024,128]{3,2,1,0:T(8,128)(2,1)}, bf16[4,1024,512]{2,1,0:T(8,128)(2,1)}, bf16[4,1024,128]{2,1,0:T(8,128)(2,1)S(1)}, f32[4,1024,128]{2,1,0:T(8,128)}) custom-call(s32[21]{0:T(128)S(1)} %concatenate.121.info_ref.refs_0_, bf16[1024,768]{1,0:T(8,128)(2,1)} %multiply_convert_fusion.x_ref, ...), custom_call_target="tpu_custom_call" | custom-call | flops 10000000000 | bytes 12000000 | tf_op jit(solution)/shard_map/attend/pallas_call | solution.py:145
  89.5 14.7 %forward_rest.1 = (f32[1024,768]{1,0:T(8,128)}, bf16[1024,768]{1,0:T(8,128)(2,1)}, bf16[8,2432]{1,0:T(8,128)(2,1)S(1)}, bf16[768,768]{1,0:T(8,128)(2,1)}, bf16[768,768]{1,0:T(8,128)(2,1)}) custom-call(s32[21]{0:T(128)S(1)} %concatenate.121.info_ref.refs_0_, f32[1024,768]{1,0:T(8,128)} %copy-done.7, f32[35,768]{1,0:T(8,128)S(1)} %reshape.477.gain_ref, ...), custom_call_target="tpu_custom_call" | custom-call | flops 10000000000 | bytes 20000000 | tf_op jit(solution)/shard_map/forward_rest/pallas_call | solution.py:406
  113.3 3.9 %collective-permute-done.18 = bf16[4,8,2432]{2,1,0:T(8,128)(2,1)S(1)} collective-permute-done((bf16[4,8,2432]{2,1,0:T(8,128)(2,1)S(1)}, bf16[4,8,2432]{2,1,0:T(8,128)(2,1)S(1)}, u32[]{:S(2)}, u32[]{:S(2)}) %collective-permute-start.18) | collective-permute-done | bytes 155680 | tf_op jit(solution)/shard_map/ppermute | solution.py:701
  118.5 5.7 %collective-permute-done.19.a3_ref = bf16[2,4,8,2432]{3,2,1,0:T(8,128)(2,1)S(1)} collective-permute-done((bf16[2,4,8,2432]{3,2,1,0:T(8,128)(2,1)S(1)}, bf16[2,4,8,2432]{3,2,1,0:T(8,128)(2,1)S(1)}, u32[]{:S(2)}, u32[]{:S(2)}) %collective-permute-start.19) | collective-permute-done | bytes 311328 | tf_op jit(solution)/shard_map/ppermute | solution.py:701
  127.1 3.4 %contrast.1 = (f32[1,1]{1,0:T(1,128)}, f32[8,768]{1,0:T(8,128)S(1)}, f32[8,768]{1,0:T(8,128)S(1)}, bf16[256,768]{1,0:T(8,128)(2,1)S(1)}, bf16[256,768]{1,0:T(8,128)(2,1)S(1)}, /*index=5*/f32[1,768]{1,0:T(1,128)S(1)}) custom-call(s32[21]{0:T(128)S(1)} %concatenate.121.info_ref.refs_0_, bf16[2,4,8,2432]{3,2,1,0:T(8,128)(2,1)S(1)} %pad_maximum_fusion.8.a1_ref, ...), custom_call_target="tpu_custom_call" | custom-call | flops 3000000000 | bytes 4000000 | tf_op jit(solution)/shard_map/contrast/pallas_call | solution.py:626
  130.5 16.1 %ffn_back.1 = (f32[1024,768]{1,0:T(8,128)}, bf16[2,768,384]{2,1,0:T(8,128)(2,1)}, f32[8,768]{1,0:T(8,128)S(1)}, bf16[4,1024,128]{2,1,0:T(8,128)(2,1)}, bf16[4,10...) custom-call(s32[21]{0:T(128)S(1)} %concatenate.121.info_ref.refs_0_, ...), custom_call_target="tpu_custom_call" | custom-call | flops 14000000000 | bytes 20000000 | tf_op jit(solution)/shard_map/ffn_back/pallas_call | solution.py:527
  147.8 17.6 %attend_back.3 = (bf16[4,768,384]{2,1,0:T(8,128)(2,1)}, bf16[4,1024,384]{2,1,0:T(8,128)(2,1)}) custom-call(bf16[768,1024]{1,0:T(8,128)(2,1)} %get-tuple-element.82.xt_ref, bf16[4,3,1024,128]{3,2,1,0:T(8,128)(2,1)} %get-tuple-element.102.qkv_ref, bf16[4,1024,512]{2,1,0:T(8,128)(2,1)} %get-tuple-element.103.p_ref, bf16[4,1024,128]{2,1,0:T(8,128)(2,1)S(1)} %copy-done.6, ...), custom_call_target="tpu_custom_call" | custom-call | flops 16000000000 | bytes 12000000 | tf_op jit(solution)/shard_map/attend_back/pallas_call | solution.py:212
  170.4 10.4 %attend_back.4 = (bf16[2,768,384]{2,1,0:T(8,128)(2,1)}, bf16[2,1024,384]{2,1,0:T(8,128)(2,1)}) custom-call(bf16[768,1024]{1,0:T(8,128)(2,1)} %get-tuple-element.82.xt_ref, bf16[4,3,1024,128]{3,2,1,0:T(8,128)(2,1)} %get-tuple-element.83.qkv_ref, bf16[4,1024,512]{2,1,0:T(8,128)(2,1)} %get-tuple-element.84.p_ref, bf16[4,1024,128]{2,1,0:T(8,128)(2,1)S(1)} %copy-done.3, ...), custom_call_target="tpu_custom_call" | custom-call | flops 8000000000 | bytes 6000000 | tf_op jit(solution)/shard_map/attend_back/pallas_call | solution.py:212
  185.6 10.7 %attend_back.5 = (bf16[2,2,4,96,384]{4,3,2,1,0:T(8,128)(2,1)}, bf16[2,1024,384]{2,1,0:T(8,128)(2,1)}) custom-call(bf16[768,1024]{1,0:T(8,128)(2,1)} %get-tuple-element.82.xt_ref, bf16[4,3,1024,128]{3,2,1,0:T(8,128)(2,1)} %get-tuple-element.83.qkv_ref, bf16[4,1024,512]{2,1,0:T(8,128)(2,1)} %get-tuple-element.84.p_ref, bf16[4,1024,128]{2,1,0:T(8,128)(2,1)S(1)} %copy-done.3, ...), custom_call_target="tpu_custom_call" | custom-call | flops 8000000000 | bytes 6000000 | tf_op jit(solution)/shard_map/attend_back/pallas_call | solution.py:212
  198.6 6.8 %first_sum.1.sum_ref = f32[1024,768]{1,0:T(8,128)} custom-call(bf16[4,1024,384]{2,1,0:T(8,128)(2,1)} %get-tuple-element.119.refs_0_, bf16[4,768,384]{2,1,0:T(8,128)(2,1)} %get-tuple-element.91.refs_3_.refs_5_.refs_1_), custom_call_target="tpu_custom_call" | custom-call | flops 7000000000 | bytes 12000000 | tf_op jit(solution)/shard_map/first_sum/pallas_call | solution.py:252
  207.9 6.2 %collective-permute-done.25 = bf16[4,144,384]{2,1,0:T(8,128)(2,1)S(1)} collective-permute-done((bf16[4,144,384]{2,1,0:T(8,128)(2,1)S(1)}, bf16[4,144,384]{2,1,0:T(8,128)(2,1)S(1)}, u32[]{:S(2)}, u32[]{:S(2)}) %collective-permute-start.25) | collective-permute-done | bytes 442400 | tf_op jit(solution)/shard_map/ppermute | solution.py:701
  219.8 8.4 %first_back.1 = f32[40,768]{1,0:T(8,128)S(1)} custom-call(f32[1024,768]{1,0:T(8,128)} %copy-done.7, f32[1024,768]{1,0:T(8,128)} %get-tuple-element.117.dmid_ref, bf16[1024,32]{1,0:T(8,128)(2,1)S(1)} %copy.82.ident_ref, f32[35,768]{1,0:T(8,128)S(1)} %reshape.477.gain_ref, f32[1024,768]{1,0:T(8,128)} %first_sum.1.sum_ref, ...), custom_call_target="tpu_custom_call" | custom-call | flops 4000000000 | bytes 10000000 | tf_op jit(solution)/shard_map/first_back/pallas_call | solution.py:300
  230.2 2.8 %collective-permute-start.33 = (bf16[96,384]{1,0:T(8,128)(2,1)S(1)}, bf16[96,384]{1,0:T(8,128)(2,1)S(1)}, u32[]{:S(2)}, u32[]{:S(2)}) collective-permute-start(bf16[96,384]{1,0:T(8,128)(2,1)S(1)} %get-tuple-element.176), channel_id=1, source_target_pairs={{0,24},{1,25},{2,26},{3,27},{4,28},{5,29},{6,30},{7,31},{8,0},{9,1... | collective-permute-start | bytes 221192 | tf_op jit(solution)/shard_map/ppermute | solution.py:701
  234.2 2.6 all-to-all-start.1
  237.8 7.1 %all-to-all-done.1 = f32[32,1,816]{2,1,0:T(1,128)S(1)} async-done(((f32[32,1,816]{2,1,0:T(1,128)}), f32[32,1,816]{2,1,0:T(1,128)S(1)}, u32[]{:S(2)}, u32[]{:S(2)}) %all-to-all-start.1) | async-done | bytes 104480 | tf_op jit(solution)/shard_map/all_to_all | solution.py:1072
  253.6 3.4 %all-to-all-done.2 = f32[32,1,128]{2,1,0:T(1,128)S(1)} async-done(((f32[32,1,128]{2,1,0:T(1,128)}), f32[32,1,128]{2,1,0:T(1,128)S(1)}, u32[]{:S(2)}, u32[]{:S(2)}) %all-to-all-start.2) | async-done | bytes 16416 | tf_op jit(solution)/shard_map/all_to_all | solution.py:1075
  257.7 3.0 %update.1 = (f32[1,1]{1,0:T(1,128)}, f32[24,32]{1,0:T(8,128)}, f32[3,96,192]{2,1,0:T(8,128)}, f32[192,96]{1,0:T(8,128)}, f32[2,24,768]{2,1,0:T(8,128)}, /*index=...) custom-call(f32[32,128]{1,0:T(8,128)} %bitcast.288, ...), custom_call_target="tpu_custom_call" | custom-call | flops 5000000 | bytes 6000000 | tf_op jit(solution)/shard_map/update/pallas_call | solution.py:896
  (213 shorter events, 82.1 us)
Async XLA Ops:
  4.6 9.7 %collective-permute-start.1 = (bf16[2,96,384]{2,1,0:T(8,128)(2,1)S(1)}, bf16[2,96,384]{2,1,0:T(8,128)(2,1)S(1)}, u32[]{:S(2)}, u32[]{:S(2)}) collective-permute-start(bf16[2,96,384]{2,1,0:T(8,128)(2,1)S(1)} %get-tuple-element.194), channel_id=1, source_target_pairs={{0,8},{1,9},{2,10},{3,11},{4,12},{5,13},{6,14},{7,15},{8,16},{9,17... | collective-permute-start | bytes 442376 | tf_op jit(solution)/shard_map/ppermute | solution.py:701
  7.6 12.6 %collective-permute-start.2 = (bf16[2,96,384]{2,1,0:T(8,128)(2,1)S(1)}, bf16[2,96,384]{2,1,0:T(8,128)(2,1)S(1)}, u32[]{:S(2)}, u32[]{:S(2)}) collective-permute-start(bf16[2,96,384]{2,1,0:T(8,128)(2,1)S(1)} %get-tuple-element.194), channel_id=1, source_target_pairs={{0,16},{1,17},{2,18},{3,19},{4,20},{5,21},{6,22},{7,23},{8,24},{9,... | collective-permute-start | bytes 442376 | tf_op jit(solution)/shard_map/ppermute | solution.py:701
  10.2 10.0 %collective-permute-start.3 = (bf16[2,96,384]{2,1,0:T(8,128)(2,1)S(1)}, bf16[2,96,384]{2,1,0:T(8,128)(2,1)S(1)}, u32[]{:S(2)}, u32[]{:S(2)}) collective-permute-start(bf16[2,96,384]{2,1,0:T(8,128)(2,1)S(1)} %get-tuple-element.194), channel_id=1, source_target_pairs={{0,24},{1,25},{2,26},{3,27},{4,28},{5,29},{6,30},{7,31},{8,0},{9,1... | collective-permute-start | bytes 442376 | tf_op jit(solution)/shard_map/ppermute | solution.py:701
  20.4 10.4 %collective-permute-start.6 = (bf16[24,768]{1,0:T(8,128)(2,1)S(1)}, bf16[24,768]{1,0:T(8,128)(2,1)S(1)}, u32[]{:S(2)}, u32[]{:S(2)}) collective-permute-start(bf16[24,768]{1,0:T(8,128)(2,1)S(1)} %dynamic-slice_bitcast_fusion.15), channel_id=1, source_target_pairs={{0,1},{1,0},{2,3},{3,2},{4,5},{5,4},{6,7},{7,6},{8,9},{9,8},{10,11... | collective-permute-start | bytes 110600 | tf_op jit(solution)/shard_map/ppermute | solution.py:701
  21.8 15.1 %all-to-all-start = ((f32[32,1,840]{2,1,0:T(1,128)}), f32[32,1,840]{2,1,0:T(1,128)S(1)}, u32[]{:S(2)}, u32[]{:S(2)}) async-start(f32[32,1,840]{2,1,0:T(1,128)} %broadcast_in_dim.24), calls=%async_computation | async-start | bytes 229376 | tf_op jit(solution)/shard_map/all_to_all | solution.py:953
  28.9 11.5 %collective-permute-start.4 = (bf16[4,2,96,384]{3,2,1,0:T(8,128)(2,1)S(1)}, bf16[4,2,96,384]{3,2,1,0:T(8,128)(2,1)S(1)}, u32[]{:S(2)}, u32[]{:S(2)}) collective-permute-start(bf16[4,2,96,384]{3,2,1,0:T(8,128)(2,1)S(1)} %pad_maximum_fusion.3), channel_id=1, source_target_pairs={{0,4},{1,3},{2,6},{3,1},{4,0},{5,7},{6,2},{7,5},{8,12},{9,11},{10,... | collective-permute-start | bytes 1769480 | tf_op jit(solution)/shard_map/ppermute | solution.py:701
  41.5 19.7 %collective-permute-start.5 = (bf16[2,4,2,96,384]{4,3,2,1,0:T(8,128)(2,1)}, bf16[2,4,2,96,384]{4,3,2,1,0:T(8,128)(2,1)}, u32[]{:S(2)}, u32[]{:S(2)}) collective-permute-start(bf16[2,4,2,96,384]{4,3,2,1,0:T(8,128)(2,1)} %pad_maximum_fusion.refs_0_), channel_id=1, source_target_pairs={{0,2},{1,5},{2,0},{3,7},{4,6},{5,1},{6,4},{7,3},{8,10},{9,13},{10,... | collective-permute-start | bytes 3538952 | tf_op jit(solution)/shard_map/ppermute | solution.py:701
  42.8 33.6 %collective-permute-start.13 = (bf16[2,4,2,96,384]{4,3,2,1,0:T(8,128)(2,1)}, bf16[2,4,2,96,384]{4,3,2,1,0:T(8,128)(2,1)}, u32[]{:S(2)}, u32[]{:S(2)}) collective-permute-start(bf16[2,4,2,96,384]{4,3,2,1,0:T(8,128)(2,1)} %pad_maximum_fusion.refs_0_), channel_id=1, source_target_pairs={{0,1},{1,0},{2,3},{3,2},{4,5},{5,4},{6,7},{7,6},{8,9},{9,8},{10,11... | collective-permute-start | bytes 3538952 | tf_op jit(solution)/shard_map/ppermute | solution.py:701
  42.8 9.9 %collective-permute-start.10 = (bf16[4,2,24,768]{3,2,1,0:T(8,128)(2,1)S(1)}, bf16[4,2,24,768]{3,2,1,0:T(8,128)(2,1)S(1)}, u32[]{:S(2)}, u32[]{:S(2)}) collective-permute-start(bf16[4,2,24,768]{3,2,1,0:T(8,128)(2,1)S(1)} %bitcast_dynamic-update-slice_fusion), channel_id=1, source_target_pairs={{0,4},{1,3},{2,6},{3,1},{4,0},{5,7},{6,2},{7,5},{8,12},{9,11},{10,... | collective-permute-start | bytes 884744 | tf_op jit(solution)/shard_map/ppermute | solution.py:701
  52.8 21.3 %collective-permute-start.11 = (bf16[2,4,2,24,768]{4,3,2,1,0:T(8,128)(2,1)S(1)}, bf16[2,4,2,24,768]{4,3,2,1,0:T(8,128)(2,1)S(1)}, u32[]{:S(2)}, u32[]{:S(2)}) collective-permute-start(bf16[2,4,2,24,768]{4,3,2,1,0:T(8,128)(2,1)S(1)} %pad_maximum_fusion.4), channel_id=1, source_target_pairs={{0,2},{1,5},{2,0},{3,7},{4,6},{5,1},{6,4},{7,3},{8,10},{9,13},{10,... | collective-permute-start | bytes 1769480 | tf_op jit(solution)/shard_map/ppermute | solution.py:701
  61.2 15.2 %collective-permute-start.14 = (bf16[2,4,2,96,384]{4,3,2,1,0:T(8,128)(2,1)}, bf16[2,4,2,96,384]{4,3,2,1,0:T(8,128)(2,1)}, u32[]{:S(2)}, u32[]{:S(2)}) collective-permute-start(bf16[2,4,2,96,384]{4,3,2,1,0:T(8,128)(2,1)} %collective-permute-done.5.refs_1_), channel_id=1, source_target_pairs={{0,1},{1,0},{2,3},{3,2},{4,5},{5,4},{6,7},{7,6},{8,9},{9,8},{10,11... | collective-permute-start | bytes 3538952 | tf_op jit(solution)/shard_map/ppermute | solution.py:701
  75.5 13.9 %collective-permute-start.12 = (bf16[768,768]{1,0:T(8,128)(2,1)}, bf16[768,768]{1,0:T(8,128)(2,1)}, u32[]{:S(2)}, u32[]{:S(2)}) collective-permute-start(bf16[768,768]{1,0:T(8,128)(2,1)} %bitcast.48.ffn_ref), channel_id=1, source_target_pairs={{0,1},{1,0},{2,3},{3,2},{4,5},{5,4},{6,7},{7,6},{8,9},{9,8},{10,11... | collective-permute-start | bytes 3538952 | tf_op jit(solution)/shard_map/ppermute | solution.py:701
  165.4 16.7 %collective-permute-start.22 = (bf16[4,768,384]{2,1,0:T(8,128)(2,1)}, bf16[4,768,384]{2,1,0:T(8,128)(2,1)}, u32[]{:S(2)}, u32[]{:S(2)}) collective-permute-start(bf16[4,768,384]{2,1,0:T(8,128)(2,1)} %get-tuple-element.106), channel_id=1, source_target_pairs={{0,1},{1,0},{2,3},{3,2},{4,5},{5,4},{6,7},{7,6},{8,9},{9,8},{10,11... | collective-permute-start | bytes 7077896 | tf_op jit(solution)/shard_map/ppermute | solution.py:701
  169.1 11.7 %collective-permute-start.23 = (bf16[2,4,2,2,24,384]{5,4,1,3,2,0:T(8,128)(2,1)}, bf16[2,4,2,2,24,384]{5,4,1,3,2,0:T(8,128)(2,1)}, u32[]{:S(2)}, u32[]{:S(2)}) collective-permute-start(bf16[2,4,2,2,24,384]{5,4,1,3,2,0:T(8,128)(2,1)} %bitcast.260), channel_id=1, source_target_pairs={{0,1},{1,0},{2,3},{3,2},{4,5},{5,4},{6,7},{7,6},{8,9},{9,8},{10,11... | collective-permute-start | bytes 1769480 | tf_op jit(solution)/shard_map/ppermute | solution.py:701
  184.3 21.1 %collective-permute-start.24 = (bf16[2,4,144,384]{3,2,1,0:T(8,128)(2,1)S(1)}, bf16[2,4,144,384]{3,2,1,0:T(8,128)(2,1)S(1)}, u32[]{:S(2)}, u32[]{:S(2)}) collective-permute-start(bf16[2,4,144,384]{3,2,1,0:T(8,128)(2,1)S(1)} %pad_maximum_fusion.2), channel_id=1, source_target_pairs={{0,2},{1,5},{2,0},{3,7},{4,6},{5,1},{6,4},{7,3},{8,10},{9,13},{10,... | collective-permute-start | bytes 2654216 | tf_op jit(solution)/shard_map/ppermute | solution.py:701
  197.7 9.9 %collective-permute-start.29 = (bf16[2,4,96,384]{3,2,1,0:T(8,128)(2,1)S(1)}, bf16[2,4,96,384]{3,2,1,0:T(8,128)(2,1)S(1)}, u32[]{:S(2)}, u32[]{:S(2)}) collective-permute-start(bf16[2,4,96,384]{3,2,1,0:T(8,128)(2,1)S(1)} %pad_maximum_fusion.5), channel_id=1, source_target_pairs={{0,2},{1,5},{2,0},{3,7},{4,6},{5,1},{6,4},{7,3},{8,10},{9,13},{10,... | collective-permute-start | bytes 1769480 | tf_op jit(solution)/shard_map/ppermute | solution.py:701
  205.7 8.4 %collective-permute-start.25 = (bf16[4,144,384]{2,1,0:T(8,128)(2,1)S(1)}, bf16[4,144,384]{2,1,0:T(8,128)(2,1)S(1)}, u32[]{:S(2)}, u32[]{:S(2)}) collective-permute-start(bf16[4,144,384]{2,1,0:T(8,128)(2,1)S(1)} %fusion.5), channel_id=1, source_target_pairs={{0,4},{1,3},{2,6},{3,1},{4,0},{5,7},{6,2},{7,5},{8,12},{9,11},{10,... | collective-permute-start | bytes 1327112 | tf_op jit(solution)/shard_map/ppermute | solution.py:701
  214.0 14.4 %collective-permute-start.30 = (bf16[4,96,384]{2,1,0:T(8,128)(2,1)S(1)}, bf16[4,96,384]{2,1,0:T(8,128)(2,1)S(1)}, u32[]{:S(2)}, u32[]{:S(2)}) collective-permute-start(bf16[4,96,384]{2,1,0:T(8,128)(2,1)S(1)} %fusion.10), channel_id=1, source_target_pairs={{0,4},{1,3},{2,6},{3,1},{4,0},{5,7},{6,2},{7,5},{8,12},{9,11},{10,... | collective-permute-start | bytes 884744 | tf_op jit(solution)/shard_map/ppermute | solution.py:701
  215.5 12.8 %collective-permute-start.26 = (bf16[144,384]{1,0:T(8,128)(2,1)S(1)}, bf16[144,384]{1,0:T(8,128)(2,1)S(1)}, u32[]{:S(2)}, u32[]{:S(2)}) collective-permute-start(bf16[144,384]{1,0:T(8,128)(2,1)S(1)} %get-tuple-element.170), channel_id=1, source_target_pairs={{0,8},{1,9},{2,10},{3,11},{4,12},{5,13},{6,14},{7,15},{8,16},{9,17... | collective-permute-start | bytes 331784 | tf_op jit(solution)/shard_map/ppermute | solution.py:701
  216.5 11.8 %collective-permute-start.27 = (bf16[144,384]{1,0:T(8,128)(2,1)S(1)}, bf16[144,384]{1,0:T(8,128)(2,1)S(1)}, u32[]{:S(2)}, u32[]{:S(2)}) collective-permute-start(bf16[144,384]{1,0:T(8,128)(2,1)S(1)} %get-tuple-element.172), channel_id=1, source_target_pairs={{0,16},{1,17},{2,18},{3,19},{4,20},{5,21},{6,22},{7,23},{8,24},{9,... | collective-permute-start | bytes 331784 | tf_op jit(solution)/shard_map/ppermute | solution.py:701
  218.8 9.5 %collective-permute-start.28 = (bf16[144,384]{1,0:T(8,128)(2,1)S(1)}, bf16[144,384]{1,0:T(8,128)(2,1)S(1)}, u32[]{:S(2)}, u32[]{:S(2)}) collective-permute-start(bf16[144,384]{1,0:T(8,128)(2,1)S(1)} %get-tuple-element.171), channel_id=1, source_target_pairs={{0,24},{1,25},{2,26},{3,27},{4,28},{5,29},{6,30},{7,31},{8,0},{9,1... | collective-permute-start | bytes 331784 | tf_op jit(solution)/shard_map/ppermute | solution.py:701
  234.2 10.6 %all-to-all-start.1 = ((f32[32,1,816]{2,1,0:T(1,128)}), f32[32,1,816]{2,1,0:T(1,128)S(1)}, u32[]{:S(2)}, u32[]{:S(2)}) async-start(f32[32,1,816]{2,1,0:T(1,128)} %all_to_all.23), calls=%async_computation.1 | async-start | bytes 229376 | tf_op jit(solution)/shard_map/all_to_all | solution.py:1072
  236.9 13.7 %collective-permute-start.34 = (f32[96,384]{1,0:T(8,128)S(1)}, f32[96,384]{1,0:T(8,128)S(1)}, u32[]{:S(2)}, u32[]{:S(2)}) collective-permute-start(f32[96,384]{1,0:T(8,128)S(1)} %fusion.14.refs_1_), channel_id=1, source_target_pairs={{0,1},{1,0},{2,3},{3,2},{4,5},{5,4},{6,7},{7,6},{8,9},{9,8},{10,11... | collective-permute-start | bytes 442376 | tf_op jit(solution)/shard_map/ppermute | solution.py:701
  247.4 9.6 %all-to-all-start.2 = ((f32[32,1,128]{2,1,0:T(1,128)}), f32[32,1,128]{2,1,0:T(1,128)S(1)}, u32[]{:S(2)}, u32[]{:S(2)}) async-start(f32[32,1,128]{2,1,0:T(1,128)} %bitcast.289), calls=%async_computation.2 | async-start | bytes 32768 | tf_op jit(solution)/shard_map/all_to_all | solution.py:1075
  (35 other events, 301.2 us)
where the time goes:
time: 262 us; the launch traced here: 261 us
  Pallas kernels  118 us (45%)
  waiting for transfers between devices  53.4 us (20%)
  starting transfers between devices  53 us (20%)
  local copies, waits for them, and re-layouts  18.1 us (7%)
  other arithmetic  14.1 us (5%)
    ppermute x35, waiting for transfers between devices, move(): return lax.ppermute(v, ('dp', 'head'), pairs)  42.1 us
    ppermute x35, starting transfers between devices, move(): return lax.ppermute(v, ('dp', 'head'), pairs)  40.8 us
    pallas_call x3, Pallas kernels, attend_back(): pl.pallas_call(functools.partial(attend_back_kernel, graphs=tokens // LEN...  38.8 us
    pallas_call x2, Pallas kernels, attend(): pl.pallas_call(functools.partial(attend_kernel, graphs=tokens // LEN, who...  25 us
    pallas_call x1, Pallas kernels, ffn_back(): pl.pallas_call(functools.partial(ffn_back_kernel, tile_graphs=tile_graphs...  16.1 us
    pallas_call x1, Pallas kernels, forward_rest(): pl.pallas_call(functools.partial(forward_kernel, tile_graphs=tile_graphs,...  14.7 us
    pallas_call x1, Pallas kernels, first_back(): pl.pallas_call(first_back_kernel, grid=(tokens // rows,), in_specs=[tile,...  8.38 us
    all_to_all x1, waiting for transfers between devices, per_device(): lax.all_to_all(rows, ('dp', 'head'), 0, 0, tiled=True)  7.06 us
  transfers between devices with their start and end apart: 38, of which 17 were waited for; matrix products, arithmetic and copies ran while one was open for 8% of the time, Pallas kernels for 24%

commit v1 on v0

--- a/solution.py
+++ b/solution.py
@@ -34,7 +34,7 @@
 V_AT = 128 - SW
 SCALE = HEAD_DIM ** (-0.5)
 LENS = 5
-VMEM_LIMIT = 52 * 2**20
+VMEM_LIMIT = 49 * 2**20
 
 
 def nn(a, b):
@@ -714,12 +714,12 @@
     def by_core(self, a, b):
         return jnp.where(self.core == 0, a, b)
 
-    def gather_outer(self, v):
+    def gather_outer(self, v, *late):
         out = jnp.zeros((self.outs,) + v.shape, v.dtype)
         out = lax.dynamic_update_index_in_dim(out, v, self.outer, 0)
         for by in range(1, self.outs):
             out = lax.dynamic_update_index_in_dim(
-                out, self.to_outer(v, by), (self.outer - by) % self.outs, 0
+                out, after(self.to_outer(v, by), *late), (self.outer - by) % self.outs, 0
             )
         return out
 
@@ -773,8 +773,8 @@
         total = kept.astype(F32) + came.astype(F32)
         return total[0], total[1].astype(dtype)
 
-    def fold_outer(self, kept, came, dtype):
-        total = (kept.astype(F32) + came.astype(F32)).astype(dtype)
+    def fold_outer(self, total, dtype):
+        total = total.astype(dtype)
         pick = lambda by: lax.dynamic_index_in_dim(
             total, (self.outer + by) % self.outs, 0, keepdims=False
         )
@@ -931,6 +931,7 @@
     place = Place()
     heads, head, dp, core = place.heads, place.head, place.dp, place.core
     tokens = features.shape[0] // heads
+    devices = place.n * heads
     graphs = tokens // LEN
     own_columns = norm_gains.shape[1]
 
@@ -948,18 +949,16 @@
     near = jnp.stack([pick(shards, core), place.to_core(pick(shards, 1 - core))])
     shard_rows = D // place.n
     aligned = shard_rows % 16 == 0
-    devices = place.n * heads
-    small = jnp.broadcast_to(after(small.reshape(1, -1), near), (devices, small.size))
+    near_own = (place.outer_list if aligned else place.gather_outer)(near)
+    small = jnp.broadcast_to(after(small.reshape(1, -1), near_own), (devices, small.size))
     small = lax.all_to_all(small, ("dp", "head"), 0, 0, tiled=True)
-    near_own = (place.outer_list if aligned else place.gather_outer)(near)
-    ffn = after(ffn_weight.astype(BF), near_own)
-    ffn_near = place.both_cores_of(pick(ffn, core), pick(ffn, 1 - core))
-    ffn_own = place.gather_outer(ffn_near)
-    near_own = after(near_own, small)
     near = jnp.stack([near_own, place.mixed(near_own, 0)])
     last = place.mixed(near, 1)
+    ffn = after(ffn_weight.astype(BF), near_own)
+    small = after(small, near)
+    ffn_near = place.both_cores_of(pick(ffn, core), pick(ffn, 1 - core))
+    ffn_own = place.gather_outer(ffn_near, near)
     near_others = place.to_core(near)
-    ffn_own = after(ffn_own, near)
     ffn_next = place.mixed(ffn_own, 0)
     ffn_last = place.mixed(jnp.stack([ffn_own, ffn_next]), 1)
     small = small.reshape(-1, small_rows, own_columns).transpose(1, 0, 2).reshape(small_rows, D)
@@ -1057,14 +1056,15 @@
     even_came = place.mixed(even_sent, 0)
     d_normed = first_sum([after(d_others, odd_sent)], ((0, (0, 1, 2, 3)),), [others])
     odd_kept, odd_sent = place.fold_near(odd_kept, odd_came, BF)
-    odd_sent = after(odd_sent, even_came)
     odd_came = place.mixed(odd_sent, 0)
-    even = place.fold_outer(even_kept, even_came, BF)
     rows = first_back(
         embedded, d_middle, ident_rows, gains, d_normed, d_even, after(d_odd, odd_sent), mine
     )
-    rows = after(rows, even, odd_came)
-    odd = place.fold_outer(odd_kept, odd_came, BF)
+    rows = after(rows, even_came, odd_came)
+    total = lambda kept, came: kept.astype(F32) + came.astype(F32)
+    both = jnp.concatenate([total(even_kept, even_came), total(odd_kept, odd_came)], axis=1)
+    both = place.fold_outer(both, BF)
+    even, odd = both[: even_kept.shape[1]], both[even_kept.shape[1] :]
     gain_rows = jnp.stack([jnp.sum(rows[2 * LAP :], axis=0), jnp.sum(gain_two, axis=0)])
     rows = jnp.concatenate([rows[: 2 * LAP], gain_rows], axis=0)
     row_count = rows.shape[0]

time: 262 us -> 250 us (0.954)
  starting transfers between devices: 53 us -> 44.4 us
  Pallas kernels: 118 us -> 112 us
  local copies, waits for them, and re-layouts: 18.1 us -> 24.1 us
  other arithmetic: 14.1 us -> 11.3 us
    ppermute x35 -> x32, starting transfers between devices: 40.8 us -> 32.1 us  [move(): return lax.ppermute(v, ('dp', 'head'), pairs)]
    dynamic_update_slice x3, local copies, waits for them, and re-layouts: 0.03 us -> 2.67 us  [gather_outer(): lax.dynamic_update_index_in_dim(out, after(self.to_outer(v, by), *late),...]
    unnamed x46 -> x61, local copies, waits for them, and re-layouts: 6.87 us -> 8.49 us
    ppermute x35 -> x32, waiting for transfers between devices: 42.1 us -> 40.5 us  [move(): return lax.ppermute(v, ('dp', 'head'), pairs)]
  transfers between devices with their start and end apart: 38 -> 35, of which waited for: 17 -> 18; matrix products, arithmetic and copies ran while one was open for 8% -> 10% of each run, Pallas kernels for 24% -> 24%
where the time goes in v1:
time: 250 us; the launch traced here: 249 us
  Pallas kernels  112 us (45%)
  waiting for transfers between devices  52 us (21%)
  starting transfers between devices  44.4 us (18%)
  local copies, waits for them, and re-layouts  24.1 us (10%)
  other arithmetic  11.3 us (5%)
  matrix products  2.52 us (1%)
    ppermute x32, waiting for transfers between devices, move(): return lax.ppermute(v, ('dp', 'head'), pairs)  40.5 us
    pallas_call x3, Pallas kernels, attend_back(): pl.pallas_call(functools.partial(attend_back_kernel, graphs=tokens // LEN...  36.3 us
    ppermute x32, starting transfers between devices, move(): return lax.ppermute(v, ('dp', 'head'), pairs)  32.1 us
    pallas_call x2, Pallas kernels, attend(): pl.pallas_call(functools.partial(attend_kernel, graphs=tokens // LEN, who...  23.7 us
    pallas_call x1, Pallas kernels, ffn_back(): pl.pallas_call(functools.partial(ffn_back_kernel, tile_graphs=tile_graphs...  16 us
    pallas_call x1, Pallas kernels, forward_rest(): pl.pallas_call(functools.partial(forward_kernel, tile_graphs=tile_graphs,...  14.3 us
    unnamed x61, local copies, waits for them, and re-layouts  8.49 us
    pallas_call x1, Pallas kernels, first_back(): pl.pallas_call(first_back_kernel, grid=(tokens // rows,), in_specs=[tile,...  7.95 us
  transfers between devices with their start and end apart: 35, of which 18 were waited for; matrix products, arithmetic and copies ran while one was open for 10% of the time, Pallas kernels for 24%

profile of v1, /device:TPU:0, one launch (start us, length us, event | category | flops | bytes accessed | tf_op | source)
XLA Modules:
  0.0 248.6 jit_solution(7469192527575152341)
XLA Ops:
  4.6 3.0 %collective-permute-start.1 = (bf16[2,96,384]{2,1,0:T(8,128)(2,1)S(1)}, bf16[2,96,384]{2,1,0:T(8,128)(2,1)S(1)}, u32[]{:S(2)}, u32[]{:S(2)}) collective-permute-start(bf16[2,96,384]{2,1,0:T(8,128)(2,1)S(1)} %get-tuple-element.197), channel_id=1, source_target_pairs={{0,8},{1,9},{2,10},{3,11},{4,12},{5,13},{6,14},{7,15},{8,16},{9,17... | collective-permute-start | bytes 442376 | tf_op jit(solution)/shard_map/ppermute | solution.py:701
  7.6 2.6 %collective-permute-start.2 = (bf16[2,96,384]{2,1,0:T(8,128)(2,1)S(1)}, bf16[2,96,384]{2,1,0:T(8,128)(2,1)S(1)}, u32[]{:S(2)}, u32[]{:S(2)}) collective-permute-start(bf16[2,96,384]{2,1,0:T(8,128)(2,1)S(1)} %get-tuple-element.197), channel_id=1, source_target_pairs={{0,16},{1,17},{2,18},{3,19},{4,20},{5,21},{6,22},{7,23},{8,24},{9,... | collective-permute-start | bytes 442376 | tf_op jit(solution)/shard_map/ppermute | solution.py:701
  14.4 5.8 %collective-permute-done.2 = bf16[2,96,384]{2,1,0:T(8,128)(2,1)S(1)} collective-permute-done((bf16[2,96,384]{2,1,0:T(8,128)(2,1)S(1)}, bf16[2,96,384]{2,1,0:T(8,128)(2,1)S(1)}, u32[]{:S(2)}, u32[]{:S(2)}) %collective-permute-start.2) | collective-permute-done | bytes 147488 | tf_op jit(solution)/shard_map/ppermute | solution.py:701
  23.4 6.1 %all-to-all-start = ((f32[32,1,840]{2,1,0:T(1,128)}), f32[32,1,840]{2,1,0:T(1,128)S(1)}, u32[]{:S(2)}, u32[]{:S(2)}) async-start(f32[32,1,840]{2,1,0:T(1,128)} %broadcast_in_dim.24), calls=%async_computation | async-start | bytes 229376 | tf_op jit(solution)/shard_map/all_to_all | solution.py:954
  30.1 3.6 %collective-permute-start.9 = (bf16[2,24,768]{2,1,0:T(8,128)(2,1)}, bf16[2,24,768]{2,1,0:T(8,128)(2,1)}, u32[]{:S(2)}, u32[]{:S(2)}) collective-permute-start(bf16[2,24,768]{2,1,0:T(8,128)(2,1)} %pad_maximum_fusion.13), channel_id=1, source_target_pairs={{0,24},{1,25},{2,26},{3,27},{4,28},{5,29},{6,30},{7,31},{8,0},{9,1... | collective-permute-start | bytes 221192 | tf_op jit(solution)/shard_map/ppermute | solution.py:701
  34.9 2.7 %all-to-all-done = f32[32,1,840]{2,1,0:T(1,128)S(1)} async-done(((f32[32,1,840]{2,1,0:T(1,128)}), f32[32,1,840]{2,1,0:T(1,128)S(1)}, u32[]{:S(2)}, u32[]{:S(2)}) %all-to-all-start) | async-done | bytes 107552 | tf_op jit(solution)/shard_map/all_to_all | solution.py:954
  51.6 3.1 %collective-permute-done.10 = bf16[4,2,24,768]{3,2,1,0:T(8,128)(2,1)S(1)} collective-permute-done((bf16[4,2,24,768]{3,2,1,0:T(8,128)(2,1)S(1)}, bf16[4,2,24,768]{3,2,1,0:T(8,128)(2,1)S(1)}, u32[]{:S(2)}, u32[]{:S(2)}) %collective-permute-start.10) | collective-permute-done | bytes 294944 | tf_op jit(solution)/shard_map/ppermute | solution.py:701
  57.9 12.1 %attend.2 = (bf16[4,768,384]{2,1,0:T(8,128)(2,1)}, bf16[4,3,1024,128]{3,2,1,0:T(8,128)(2,1)}, bf16[4,1024,512]{2,1,0:T(8,128)(2,1)}, bf16[4,1024,128]{2,1,0:T(8,...) custom-call(s32[21]{0:T(128)S(1)} %concatenate.125.info_ref.refs_0_, ...), custom_call_target="tpu_custom_call" | custom-call | flops 10000000000 | bytes 12000000 | tf_op jit(solution)/shard_map/attend/pallas_call | solution.py:145
  75.4 11.6 %attend.3 = (bf16[4,768,384]{2,1,0:T(8,128)(2,1)}, bf16[4,3,1024,128]{3,2,1,0:T(8,128)(2,1)}, bf16[4,1024,512]{2,1,0:T(8,128)(2,1)}, bf16[4,1024,128]{2,1,0:T(8,128)(2,1)S(1)}, f32[4,1024,128]{2,1,0:T(8,128)}) custom-call(s32[21]{0:T(128)S(1)} %concatenate.125.info_ref.refs_0_, bf16[1024,768]{1,0:T(8,128)(2,1)S(1)} %copy-done.2, ...), custom_call_target="tpu_custom_call" | custom-call | flops 10000000000 | bytes 12000000 | tf_op jit(solution)/shard_map/attend/pallas_call | solution.py:145
  87.1 14.3 %forward_rest.1 = (f32[1024,768]{1,0:T(8,128)}, bf16[1024,768]{1,0:T(8,128)(2,1)}, bf16[8,2432]{1,0:T(8,128)(2,1)S(1)}, bf16[768,768]{1,0:T(8,128)(2,1)S(1)}, bf16[768,768]{1,0:T(8,128)(2,1)S(1)}) custom-call(s32[21]{0:T(128)S(1)} %concatenate.125.info_ref.refs_0_, f32[1024,768]{1,0:T(8,128)} %copy-done.14, f32[35,768]{1,0:T(8,128)S(1)} %reshape.474.gain_ref, ...), custom_call_target="tpu_custom_call" | custom-call | flops 10000000000 | bytes 20000000 | tf_op jit(solution)/shard_map/forward_rest/pallas_call | solution.py:406
  108.9 4.5 %collective-permute-done.18 = bf16[4,8,2432]{2,1,0:T(8,128)(2,1)S(1)} collective-permute-done((bf16[4,8,2432]{2,1,0:T(8,128)(2,1)S(1)}, bf16[4,8,2432]{2,1,0:T(8,128)(2,1)S(1)}, u32[]{:S(2)}, u32[]{:S(2)}) %collective-permute-start.18) | collective-permute-done | bytes 155680 | tf_op jit(solution)/shard_map/ppermute | solution.py:701
  114.0 6.4 %collective-permute-done.19.a3_ref = bf16[2,4,8,2432]{3,2,1,0:T(8,128)(2,1)S(1)} collective-permute-done((bf16[2,4,8,2432]{3,2,1,0:T(8,128)(2,1)S(1)}, bf16[2,4,8,2432]{3,2,1,0:T(8,128)(2,1)S(1)}, u32[]{:S(2)}, u32[]{:S(2)}) %collective-permute-start.19) | collective-permute-done | bytes 311328 | tf_op jit(solution)/shard_map/ppermute | solution.py:701
  122.0 3.4 %contrast.1 = (f32[1,1]{1,0:T(1,128)}, f32[8,768]{1,0:T(8,128)S(1)}, f32[8,768]{1,0:T(8,128)S(1)}, bf16[256,768]{1,0:T(8,128)(2,1)S(1)}, bf16[256,768]{1,0:T(8,128)(2,1)S(1)}, /*index=5*/f32[1,768]{1,0:T(1,128)S(1)}) custom-call(s32[21]{0:T(128)S(1)} %concatenate.125.info_ref.refs_0_, bf16[2,4,8,2432]{3,2,1,0:T(8,128)(2,1)S(1)} %pad_maximum_fusion.8.a1_ref, ...), custom_call_target="tpu_custom_call" | custom-call | flops 3000000000 | bytes 4000000 | tf_op jit(solution)/shard_map/contrast/pallas_call | solution.py:626
  125.4 16.0 %ffn_back.1 = (f32[1024,768]{1,0:T(8,128)}, bf16[2,768,384]{2,1,0:T(8,128)(2,1)}, f32[8,768]{1,0:T(8,128)S(1)}, bf16[4,1024,128]{2,1,0:T(8,128)(2,1)S(1)}, bf16[...) custom-call(s32[21]{0:T(128)S(1)} %concatenate.125.info_ref.refs_0_, ...), custom_call_target="tpu_custom_call" | custom-call | flops 14000000000 | bytes 20000000 | tf_op jit(solution)/shard_map/ffn_back/pallas_call | solution.py:527
  143.3 16.9 %attend_back.3 = (bf16[4,768,384]{2,1,0:T(8,128)(2,1)}, bf16[4,1024,384]{2,1,0:T(8,128)(2,1)}) custom-call(bf16[768,1024]{1,0:T(8,128)(2,1)S(1)} %copy-done.5, bf16[4,3,1024,128]{3,2,1,0:T(8,128)(2,1)} %get-tuple-element.107.qkv_ref, bf16[4,1024,512]{2,1,0:T(8,128)(2,1)} %get-tuple-element.108.p_ref, bf16[4,1024,128]{2,1,0:T(8,128)(2,1)S(1)} %get-tuple-element.109.aug_ref, ...), custom_call_target="tpu_custom_call" | custom-call | flops 16000000000 | bytes 12000000 | tf_op jit(solution)/shard_map/attend_back/pallas_call | solution.py:212
  165.5 9.5 %attend_back.4 = (bf16[2,768,384]{2,1,0:T(8,128)(2,1)S(1)}, bf16[2,1024,384]{2,1,0:T(8,128)(2,1)S(1)}) custom-call(bf16[768,1024]{1,0:T(8,128)(2,1)} %copy-done.4, bf16[4,3,1024,128]{3,2,1,0:T(8,128)(2,1)} %get-tuple-element.86.qkv_ref, bf16[4,1024,512]{2,1,0:T(8,128)(2,1)} %get-tuple-element.87.p_ref, bf16[4,1024,128]{2,1,0:T(8,128)(2,1)S(1)} %copy-done.7, ...), custom_call_target="tpu_custom_call" | custom-call | flops 8000000000 | bytes 6000000 | tf_op jit(solution)/shard_map/attend_back/pallas_call | solution.py:212
  179.0 9.8 %attend_back.5 = (bf16[2,2,4,96,384]{4,3,2,1,0:T(8,128)(2,1)S(1)}, bf16[2,1024,384]{2,1,0:T(8,128)(2,1)S(1)}) custom-call(bf16[768,1024]{1,0:T(8,128)(2,1)} %copy-done.4, bf16[4,3,1024,128]{3,2,1,0:T(8,128)(2,1)} %get-tuple-element.86.qkv_ref, bf16[4,1024,512]{2,1,0:T(8,128)(2,1)} %get-tuple-element.87.p_ref, bf16[4,1024,128]{2,1,0:T(8,128)(2,1)S(1)} %copy-done.7, ...), custom_call_target="tpu_custom_call" | custom-call | flops 8000000000 | bytes 6000000 | tf_op jit(solution)/shard_map/attend_back/pallas_call | solution.py:212
  190.6 6.0 %first_sum.1.sum_ref = f32[1024,768]{1,0:T(8,128)} custom-call(bf16[4,1024,384]{2,1,0:T(8,128)(2,1)} %get-tuple-element.123.refs_0_, bf16[4,768,384]{2,1,0:T(8,128)(2,1)S(1)} %copy-done.3), custom_call_target="tpu_custom_call" | custom-call | flops 7000000000 | bytes 12000000 | tf_op jit(solution)/shard_map/first_sum/pallas_call | solution.py:252
  201.6 8.0 %first_back.1 = f32[40,768]{1,0:T(8,128)S(1)} custom-call(f32[1024,768]{1,0:T(8,128)} %copy-done.14, f32[1024,768]{1,0:T(8,128)} %get-tuple-element.121.dmid_ref, bf16[1024,32]{1,0:T(8,128)(2,1)S(1)} %copy.82.ident_ref, f32[35,768]{1,0:T(8,128)S(1)} %reshape.474.gain_ref, f32[1024,768]{1,0:T(8,128)} %first_sum.1.sum_ref, ...), custom_call_target="tpu_custom_call" | custom-call | flops 4000000000 | bytes 10000000 | tf_op jit(solution)/shard_map/first_back/pallas_call | solution.py:300
  216.1 3.6 %all-to-all-start.1 = ((f32[32,1,816]{2,1,0:T(1,128)}), f32[32,1,816]{2,1,0:T(1,128)S(1)}, u32[]{:S(2)}, u32[]{:S(2)}) async-start(f32[32,1,816]{2,1,0:T(1,128)} %all_to_all.26), calls=%async_computation.1 | async-start | bytes 229376 | tf_op jit(solution)/shard_map/all_to_all | solution.py:1072
  220.4 5.9 %collective-permute-done.29 = bf16[240,384]{1,0:T(8,128)(2,1)S(1)} collective-permute-done((bf16[240,384]{1,0:T(8,128)(2,1)S(1)}, bf16[240,384]{1,0:T(8,128)(2,1)S(1)}, u32[]{:S(2)}, u32[]{:S(2)}) %collective-permute-start.29) | collective-permute-done | bytes 184352 | tf_op jit(solution)/shard_map/ppermute | solution.py:701
  227.9 4.6 %all-to-all-done.1 = f32[32,1,816]{2,1,0:T(1,128)S(1)} async-done(((f32[32,1,816]{2,1,0:T(1,128)}), f32[32,1,816]{2,1,0:T(1,128)S(1)}, u32[]{:S(2)}, u32[]{:S(2)}) %all-to-all-start.1) | async-done | bytes 104480 | tf_op jit(solution)/shard_map/all_to_all | solution.py:1072
  240.4 4.3 %all-to-all-done.2 = f32[32,1,128]{2,1,0:T(1,128)S(1)} async-done(((f32[32,1,128]{2,1,0:T(1,128)}), f32[32,1,128]{2,1,0:T(1,128)S(1)}, u32[]{:S(2)}, u32[]{:S(2)}) %all-to-all-start.2) | async-done | bytes 16416 | tf_op jit(solution)/shard_map/all_to_all | solution.py:1075
  245.3 3.0 %update.1 = (f32[1,1]{1,0:T(1,128)}, f32[24,32]{1,0:T(8,128)}, f32[3,96,192]{2,1,0:T(8,128)}, f32[192,96]{1,0:T(8,128)}, f32[2,24,768]{2,1,0:T(8,128)}, /*index=...) custom-call(f32[32,128]{1,0:T(8,128)} %bitcast.285, ...), custom_call_target="tpu_custom_call" | custom-call | flops 5000000 | bytes 6000000 | tf_op jit(solution)/shard_map/update/pallas_call | solution.py:896
  (221 shorter events, 79.9 us)
Async XLA Ops:
  4.6 9.7 %collective-permute-start.1 = (bf16[2,96,384]{2,1,0:T(8,128)(2,1)S(1)}, bf16[2,96,384]{2,1,0:T(8,128)(2,1)S(1)}, u32[]{:S(2)}, u32[]{:S(2)}) collective-permute-start(bf16[2,96,384]{2,1,0:T(8,128)(2,1)S(1)} %get-tuple-element.197), channel_id=1, source_target_pairs={{0,8},{1,9},{2,10},{3,11},{4,12},{5,13},{6,14},{7,15},{8,16},{9,17... | collective-permute-start | bytes 442376 | tf_op jit(solution)/shard_map/ppermute | solution.py:701
  7.6 12.6 %collective-permute-start.2 = (bf16[2,96,384]{2,1,0:T(8,128)(2,1)S(1)}, bf16[2,96,384]{2,1,0:T(8,128)(2,1)S(1)}, u32[]{:S(2)}, u32[]{:S(2)}) collective-permute-start(bf16[2,96,384]{2,1,0:T(8,128)(2,1)S(1)} %get-tuple-element.197), channel_id=1, source_target_pairs={{0,16},{1,17},{2,18},{3,19},{4,20},{5,21},{6,22},{7,23},{8,24},{9,... | collective-permute-start | bytes 442376 | tf_op jit(solution)/shard_map/ppermute | solution.py:701
  10.2 10.0 %collective-permute-start.3 = (bf16[2,96,384]{2,1,0:T(8,128)(2,1)S(1)}, bf16[2,96,384]{2,1,0:T(8,128)(2,1)S(1)}, u32[]{:S(2)}, u32[]{:S(2)}) collective-permute-start(bf16[2,96,384]{2,1,0:T(8,128)(2,1)S(1)} %get-tuple-element.197), channel_id=1, source_target_pairs={{0,24},{1,25},{2,26},{3,27},{4,28},{5,29},{6,30},{7,31},{8,0},{9,1... | collective-permute-start | bytes 442376 | tf_op jit(solution)/shard_map/ppermute | solution.py:701
  20.4 17.9 %collective-permute-start.4 = (bf16[4,2,96,384]{3,2,1,0:T(8,128)(2,1)S(1)}, bf16[4,2,96,384]{3,2,1,0:T(8,128)(2,1)S(1)}, u32[]{:S(2)}, u32[]{:S(2)}) collective-permute-start(bf16[4,2,96,384]{3,2,1,0:T(8,128)(2,1)S(1)} %get-tuple-element.178), channel_id=1, source_target_pairs={{0,4},{1,3},{2,6},{3,1},{4,0},{5,7},{6,2},{7,5},{8,12},{9,11},{10,... | collective-permute-start | bytes 1769480 | tf_op jit(solution)/shard_map/ppermute | solution.py:701
  23.4 14.2 %all-to-all-start = ((f32[32,1,840]{2,1,0:T(1,128)}), f32[32,1,840]{2,1,0:T(1,128)S(1)}, u32[]{:S(2)}, u32[]{:S(2)}) async-start(f32[32,1,840]{2,1,0:T(1,128)} %broadcast_in_dim.24), calls=%async_computation | async-start | bytes 229376 | tf_op jit(solution)/shard_map/all_to_all | solution.py:954
  30.1 9.8 %collective-permute-start.9 = (bf16[2,24,768]{2,1,0:T(8,128)(2,1)}, bf16[2,24,768]{2,1,0:T(8,128)(2,1)}, u32[]{:S(2)}, u32[]{:S(2)}) collective-permute-start(bf16[2,24,768]{2,1,0:T(8,128)(2,1)} %pad_maximum_fusion.13), channel_id=1, source_target_pairs={{0,24},{1,25},{2,26},{3,27},{4,28},{5,29},{6,30},{7,31},{8,0},{9,1... | collective-permute-start | bytes 221192 | tf_op jit(solution)/shard_map/ppermute | solution.py:701
  38.4 19.5 %collective-permute-start.5 = (bf16[2,4,2,96,384]{4,3,2,1,0:T(8,128)(2,1)S(1)}, bf16[2,4,2,96,384]{4,3,2,1,0:T(8,128)(2,1)}, u32[]{:S(2)}, u32[]{:S(2)}) collective-permute-start(bf16[2,4,2,96,384]{4,3,2,1,0:T(8,128)(2,1)S(1)} %pad_maximum_fusion.refs_0_), channel_id=1, source_target_pairs={{0,2},{1,5},{2,0},{3,7},{4,6},{5,1},{6,4},{7,3},{8,10},{9,13},{10,... | collective-permute-start | bytes 3538952 | tf_op jit(solution)/shard_map/ppermute | solution.py:701
  38.7 36.6 %collective-permute-start.13 = (bf16[2,4,2,96,384]{4,3,2,1,0:T(8,128)(2,1)S(1)}, bf16[2,4,2,96,384]{4,3,2,1,0:T(8,128)(2,1)}, u32[]{:S(2)}, u32[]{:S(2)}) collective-permute-start(bf16[2,4,2,96,384]{4,3,2,1,0:T(8,128)(2,1)S(1)} %pad_maximum_fusion.refs_0_), channel_id=1, source_target_pairs={{0,1},{1,0},{2,3},{3,2},{4,5},{5,4},{6,7},{7,6},{8,9},{9,8},{10,11... | collective-permute-start | bytes 3538952 | tf_op jit(solution)/shard_map/ppermute | solution.py:701
  44.8 9.9 %collective-permute-start.10 = (bf16[4,2,24,768]{3,2,1,0:T(8,128)(2,1)S(1)}, bf16[4,2,24,768]{3,2,1,0:T(8,128)(2,1)S(1)}, u32[]{:S(2)}, u32[]{:S(2)}) collective-permute-start(bf16[4,2,24,768]{3,2,1,0:T(8,128)(2,1)S(1)} %bitcast_dynamic-update-slice_fusion), channel_id=1, source_target_pairs={{0,4},{1,3},{2,6},{3,1},{4,0},{5,7},{6,2},{7,5},{8,12},{9,11},{10,... | collective-permute-start | bytes 884744 | tf_op jit(solution)/shard_map/ppermute | solution.py:701
  54.8 15.2 %collective-permute-start.11 = (bf16[2,4,2,24,768]{4,3,2,1,0:T(8,128)(2,1)S(1)}, bf16[2,4,2,24,768]{4,3,2,1,0:T(8,128)(2,1)S(1)}, u32[]{:S(2)}, u32[]{:S(2)}) collective-permute-start(bf16[2,4,2,24,768]{4,3,2,1,0:T(8,128)(2,1)S(1)} %pad_maximum_fusion.4), channel_id=1, source_target_pairs={{0,2},{1,5},{2,0},{3,7},{4,6},{5,1},{6,4},{7,3},{8,10},{9,13},{10,... | collective-permute-start | bytes 1769480 | tf_op jit(solution)/shard_map/ppermute | solution.py:701
  57.9 17.5 %collective-permute-start.14 = (bf16[2,4,2,96,384]{4,3,2,1,0:T(8,128)(2,1)}, bf16[2,4,2,96,384]{4,3,2,1,0:T(8,128)(2,1)}, u32[]{:S(2)}, u32[]{:S(2)}) collective-permute-start(bf16[2,4,2,96,384]{4,3,2,1,0:T(8,128)(2,1)} %collective-permute-done.5.refs_1_), channel_id=1, source_target_pairs={{0,1},{1,0},{2,3},{3,2},{4,5},{5,4},{6,7},{7,6},{8,9},{9,8},{10,11... | collective-permute-start | bytes 3538952 | tf_op jit(solution)/shard_map/ppermute | solution.py:701
  72.6 14.5 %collective-permute-start.12 = (bf16[768,768]{1,0:T(8,128)(2,1)}, bf16[768,768]{1,0:T(8,128)(2,1)}, u32[]{:S(2)}, u32[]{:S(2)}) collective-permute-start(bf16[768,768]{1,0:T(8,128)(2,1)} %bitcast.48.ffn_ref), channel_id=1, source_target_pairs={{0,1},{1,0},{2,3},{3,2},{4,5},{5,4},{6,7},{7,6},{8,9},{9,8},{10,11... | collective-permute-start | bytes 3538952 | tf_op jit(solution)/shard_map/ppermute | solution.py:701
  160.2 16.1 %collective-permute-start.22 = (bf16[4,768,384]{2,1,0:T(8,128)(2,1)}, bf16[4,768,384]{2,1,0:T(8,128)(2,1)}, u32[]{:S(2)}, u32[]{:S(2)}) collective-permute-start(bf16[4,768,384]{2,1,0:T(8,128)(2,1)} %get-tuple-element.111), channel_id=1, source_target_pairs={{0,1},{1,0},{2,3},{3,2},{4,5},{5,4},{6,7},{7,6},{8,9},{9,8},{10,11... | collective-permute-start | bytes 7077896 | tf_op jit(solution)/shard_map/ppermute | solution.py:701
  163.1 12.0 %collective-permute-start.23 = (bf16[2,4,2,2,24,384]{5,4,1,3,2,0:T(8,128)(2,1)}, bf16[2,4,2,2,24,384]{5,4,1,3,2,0:T(8,128)(2,1)}, u32[]{:S(2)}, u32[]{:S(2)}) collective-permute-start(bf16[2,4,2,2,24,384]{5,4,1,3,2,0:T(8,128)(2,1)} %bitcast.256), channel_id=1, source_target_pairs={{0,1},{1,0},{2,3},{3,2},{4,5},{5,4},{6,7},{7,6},{8,9},{9,8},{10,11... | collective-permute-start | bytes 1769480 | tf_op jit(solution)/shard_map/ppermute | solution.py:701
  178.4 22.4 %collective-permute-start.24 = (bf16[2,4,144,384]{3,2,1,0:T(8,128)(2,1)S(1)}, bf16[2,4,144,384]{3,2,1,0:T(8,128)(2,1)S(1)}, u32[]{:S(2)}, u32[]{:S(2)}) collective-permute-start(bf16[2,4,144,384]{3,2,1,0:T(8,128)(2,1)S(1)} %pad_maximum_fusion.2), channel_id=1, source_target_pairs={{0,2},{1,5},{2,0},{3,7},{4,6},{5,1},{6,4},{7,3},{8,10},{9,13},{10,... | collective-permute-start | bytes 2654216 | tf_op jit(solution)/shard_map/ppermute | solution.py:701
  189.1 9.9 %collective-permute-start.26 = (bf16[2,4,96,384]{3,2,1,0:T(8,128)(2,1)S(1)}, bf16[2,4,96,384]{3,2,1,0:T(8,128)(2,1)S(1)}, u32[]{:S(2)}, u32[]{:S(2)}) collective-permute-start(bf16[2,4,96,384]{3,2,1,0:T(8,128)(2,1)S(1)} %pad_maximum_fusion.5), channel_id=1, source_target_pairs={{0,2},{1,5},{2,0},{3,7},{4,6},{5,1},{6,4},{7,3},{8,10},{9,13},{10,... | collective-permute-start | bytes 1769480 | tf_op jit(solution)/shard_map/ppermute | solution.py:701
  199.2 10.4 %collective-permute-start.27 = (bf16[4,96,384]{2,1,0:T(8,128)(2,1)S(1)}, bf16[4,96,384]{2,1,0:T(8,128)(2,1)S(1)}, u32[]{:S(2)}, u32[]{:S(2)}) collective-permute-start(bf16[4,96,384]{2,1,0:T(8,128)(2,1)S(1)} %fusion.12), channel_id=1, source_target_pairs={{0,4},{1,3},{2,6},{3,1},{4,0},{5,7},{6,2},{7,5},{8,12},{9,11},{10,... | collective-permute-start | bytes 884744 | tf_op jit(solution)/shard_map/ppermute | solution.py:701
  201.0 9.7 %collective-permute-start.25 = (bf16[4,144,384]{2,1,0:T(8,128)(2,1)S(1)}, bf16[4,144,384]{2,1,0:T(8,128)(2,1)S(1)}, u32[]{:S(2)}, u32[]{:S(2)}) collective-permute-start(bf16[4,144,384]{2,1,0:T(8,128)(2,1)S(1)} %fusion.5), channel_id=1, source_target_pairs={{0,4},{1,3},{2,6},{3,1},{4,0},{5,7},{6,2},{7,5},{8,12},{9,11},{10,... | collective-permute-start | bytes 1327112 | tf_op jit(solution)/shard_map/ppermute | solution.py:701
  210.9 9.5 %collective-permute-start.28 = (bf16[240,384]{1,0:T(8,128)(2,1)S(1)}, bf16[240,384]{1,0:T(8,128)(2,1)S(1)}, u32[]{:S(2)}, u32[]{:S(2)}) collective-permute-start(bf16[240,384]{1,0:T(8,128)(2,1)S(1)} %get-tuple-element.162), channel_id=1, source_target_pairs={{0,8},{1,9},{2,10},{3,11},{4,12},{5,13},{6,14},{7,15},{8,16},{9,17... | collective-permute-start | bytes 552968 | tf_op jit(solution)/shard_map/ppermute | solution.py:701
  212.5 13.8 %collective-permute-start.29 = (bf16[240,384]{1,0:T(8,128)(2,1)S(1)}, bf16[240,384]{1,0:T(8,128)(2,1)S(1)}, u32[]{:S(2)}, u32[]{:S(2)}) collective-permute-start(bf16[240,384]{1,0:T(8,128)(2,1)S(1)} %get-tuple-element.163), channel_id=1, source_target_pairs={{0,16},{1,17},{2,18},{3,19},{4,20},{5,21},{6,22},{7,23},{8,24},{9,... | collective-permute-start | bytes 552968 | tf_op jit(solution)/shard_map/ppermute | solution.py:701
  214.3 12.1 %collective-permute-start.30 = (bf16[240,384]{1,0:T(8,128)(2,1)S(1)}, bf16[240,384]{1,0:T(8,128)(2,1)S(1)}, u32[]{:S(2)}, u32[]{:S(2)}) collective-permute-start(bf16[240,384]{1,0:T(8,128)(2,1)S(1)} %get-tuple-element.164), channel_id=1, source_target_pairs={{0,24},{1,25},{2,26},{3,27},{4,28},{5,29},{6,30},{7,31},{8,0},{9,1... | collective-permute-start | bytes 552968 | tf_op jit(solution)/shard_map/ppermute | solution.py:701
  216.1 16.4 %all-to-all-start.1 = ((f32[32,1,816]{2,1,0:T(1,128)}), f32[32,1,816]{2,1,0:T(1,128)S(1)}, u32[]{:S(2)}, u32[]{:S(2)}) async-start(f32[32,1,816]{2,1,0:T(1,128)} %all_to_all.26), calls=%async_computation.1 | async-start | bytes 229376 | tf_op jit(solution)/shard_map/all_to_all | solution.py:1072
  226.5 11.8 %collective-permute-start.31 = (f32[96,384]{1,0:T(8,128)S(1)}, f32[96,384]{1,0:T(8,128)S(1)}, u32[]{:S(2)}, u32[]{:S(2)}) collective-permute-start(f32[96,384]{1,0:T(8,128)S(1)} %slice.268.refs_1_), channel_id=1, source_target_pairs={{0,1},{1,0},{2,3},{3,2},{4,5},{5,4},{6,7},{7,6},{8,9},{9,8},{10,11... | collective-permute-start | bytes 442376 | tf_op jit(solution)/shard_map/ppermute | solution.py:701
  235.1 9.6 %all-to-all-start.2 = ((f32[32,1,128]{2,1,0:T(1,128)}), f32[32,1,128]{2,1,0:T(1,128)S(1)}, u32[]{:S(2)}, u32[]{:S(2)}) async-start(f32[32,1,128]{2,1,0:T(1,128)} %bitcast.286), calls=%async_computation.2 | async-start | bytes 32768 | tf_op jit(solution)/shard_map/all_to_all | solution.py:1075
  (39 other events, 360.6 us)

commit v2 on v1

--- a/solution.py
+++ b/solution.py
@@ -34,7 +34,7 @@
 V_AT = 128 - SW
 SCALE = HEAD_DIM ** (-0.5)
 LENS = 5
-VMEM_LIMIT = 49 * 2**20
+VMEM_LIMIT = 48 * 2**20
 
 
 def nn(a, b):
@@ -398,7 +398,7 @@
 def forward_rest(info, embedded, gains, w_up, w_down, outs, weights):
     tokens = embedded.shape[0]
     graphs = tokens // LEN
-    tile_graphs = min(2, graphs)
+    tile_graphs = min(4, graphs)
     rows = tile_graphs * LEN
     waves, groups = len(outs), outs[0].shape[0]
     full = lambda a: pl.BlockSpec(a.shape, lambda i: (0,) * a.ndim)

time: 250 us -> 249 us (level)
  Pallas kernels: 112 us -> 108 us
    unnamed x61 -> x65, local copies, waits for them, and re-layouts: 8.49 us -> 10.5 us
  transfers between devices with their start and end apart: 35 -> 35, of which waited for: 18 -> 18; matrix products, arithmetic and copies ran while one was open for 10% -> 10% of each run, Pallas kernels for 24% -> 22%
where the time goes in v2:
time: 249 us; the launch traced here: 248 us
  Pallas kernels  108 us (43%)
  waiting for transfers between devices  53.3 us (21%)
  starting transfers between devices  44.3 us (18%)
  local copies, waits for them, and re-layouts  26 us (10%)
  other arithmetic  12.3 us (5%)
  matrix products  2.52 us (1%)
    ppermute x32, waiting for transfers between devices, move(): return lax.ppermute(v, ('dp', 'head'), pairs)  41.5 us
    pallas_call x3, Pallas kernels, attend_back(): pl.pallas_call(functools.partial(attend_back_kernel, graphs=tokens // LEN...  34.6 us
    ppermute x32, starting transfers between devices, move(): return lax.ppermute(v, ('dp', 'head'), pairs)  32.1 us
    pallas_call x2, Pallas kernels, attend(): pl.pallas_call(functools.partial(attend_kernel, graphs=tokens // LEN, who...  23.7 us
    pallas_call x1, Pallas kernels, ffn_back(): pl.pallas_call(functools.partial(ffn_back_kernel, tile_graphs=tile_graphs...  16 us
    pallas_call x1, Pallas kernels, forward_rest(): pl.pallas_call(functools.partial(forward_kernel, tile_graphs=tile_graphs,...  13.3 us
    unnamed x65, local copies, waits for them, and re-layouts  10.5 us
    pallas_call x1, Pallas kernels, first_back(): pl.pallas_call(first_back_kernel, grid=(tokens // rows,), in_specs=[tile,...  7.14 us
  transfers between devices with their start and end apart: 35, of which 18 were waited for; matrix products, arithmetic and copies ran while one was open for 10% of the time, Pallas kernels for 22%

profile of v2, /device:TPU:0, one launch (start us, length us, event | category | flops | bytes accessed | tf_op | source)
XLA Modules:
  0.0 248.1 jit_solution(11613547227884017627)
XLA Ops:
  4.6 3.0 %collective-permute-start.1 = (bf16[2,96,384]{2,1,0:T(8,128)(2,1)S(1)}, bf16[2,96,384]{2,1,0:T(8,128)(2,1)S(1)}, u32[]{:S(2)}, u32[]{:S(2)}) collective-permute-start(bf16[2,96,384]{2,1,0:T(8,128)(2,1)S(1)} %get-tuple-element.197), channel_id=1, source_target_pairs={{0,8},{1,9},{2,10},{3,11},{4,12},{5,13},{6,14},{7,15},{8,16},{9,17... | collective-permute-start | bytes 442376 | tf_op jit(solution)/shard_map/ppermute | solution.py:701
  14.4 5.8 %collective-permute-done.2 = bf16[2,96,384]{2,1,0:T(8,128)(2,1)S(1)} collective-permute-done((bf16[2,96,384]{2,1,0:T(8,128)(2,1)S(1)}, bf16[2,96,384]{2,1,0:T(8,128)(2,1)S(1)}, u32[]{:S(2)}, u32[]{:S(2)}) %collective-permute-start.2) | collective-permute-done | bytes 147488 | tf_op jit(solution)/shard_map/ppermute | solution.py:701
  23.4 6.1 %all-to-all-start = ((f32[32,1,840]{2,1,0:T(1,128)}), f32[32,1,840]{2,1,0:T(1,128)S(1)}, u32[]{:S(2)}, u32[]{:S(2)}) async-start(f32[32,1,840]{2,1,0:T(1,128)} %broadcast_in_dim.24), calls=%async_computation | async-start | bytes 229376 | tf_op jit(solution)/shard_map/all_to_all | solution.py:954
  30.1 3.6 %collective-permute-start.9 = (bf16[2,24,768]{2,1,0:T(8,128)(2,1)}, bf16[2,24,768]{2,1,0:T(8,128)(2,1)}, u32[]{:S(2)}, u32[]{:S(2)}) collective-permute-start(bf16[2,24,768]{2,1,0:T(8,128)(2,1)} %pad_maximum_fusion.13), channel_id=1, source_target_pairs={{0,24},{1,25},{2,26},{3,27},{4,28},{5,29},{6,30},{7,31},{8,0},{9,1... | collective-permute-start | bytes 221192 | tf_op jit(solution)/shard_map/ppermute | solution.py:701
  34.9 2.7 %all-to-all-done = f32[32,1,840]{2,1,0:T(1,128)S(1)} async-done(((f32[32,1,840]{2,1,0:T(1,128)}), f32[32,1,840]{2,1,0:T(1,128)S(1)}, u32[]{:S(2)}, u32[]{:S(2)}) %all-to-all-start) | async-done | bytes 107552 | tf_op jit(solution)/shard_map/all_to_all | solution.py:954
  51.6 3.1 %collective-permute-done.10 = bf16[4,2,24,768]{3,2,1,0:T(8,128)(2,1)S(1)} collective-permute-done((bf16[4,2,24,768]{3,2,1,0:T(8,128)(2,1)S(1)}, bf16[4,2,24,768]{3,2,1,0:T(8,128)(2,1)S(1)}, u32[]{:S(2)}, u32[]{:S(2)}) %collective-permute-start.10) | collective-permute-done | bytes 294944 | tf_op jit(solution)/shard_map/ppermute | solution.py:701
  57.9 12.1 %attend.2 = (bf16[4,768,384]{2,1,0:T(8,128)(2,1)}, bf16[4,3,1024,128]{3,2,1,0:T(8,128)(2,1)}, bf16[4,1024,512]{2,1,0:T(8,128)(2,1)}, bf16[4,1024,128]{2,1,0:T(8,...) custom-call(s32[21]{0:T(128)S(1)} %concatenate.125.info_ref.refs_0_, ...), custom_call_target="tpu_custom_call" | custom-call | flops 10000000000 | bytes 12000000 | tf_op jit(solution)/shard_map/attend/pallas_call | solution.py:145
  75.4 11.6 %attend.3 = (bf16[4,768,384]{2,1,0:T(8,128)(2,1)}, bf16[4,3,1024,128]{3,2,1,0:T(8,128)(2,1)}, bf16[4,1024,512]{2,1,0:T(8,128)(2,1)}, bf16[4,1024,128]{2,1,0:T(8,128)(2,1)S(1)}, f32[4,1024,128]{2,1,0:T(8,128)}) custom-call(s32[21]{0:T(128)S(1)} %concatenate.125.info_ref.refs_0_, bf16[1024,768]{1,0:T(8,128)(2,1)S(1)} %copy-done.4, ...), custom_call_target="tpu_custom_call" | custom-call | flops 10000000000 | bytes 12000000 | tf_op jit(solution)/shard_map/attend/pallas_call | solution.py:145
  87.1 13.3 %forward_rest.1 = (f32[1024,768]{1,0:T(8,128)}, bf16[1024,768]{1,0:T(8,128)(2,1)}, bf16[8,2432]{1,0:T(8,128)(2,1)S(1)}, bf16[768,768]{1,0:T(8,128)(2,1)S(1)}, bf16[768,768]{1,0:T(8,128)(2,1)S(1)}) custom-call(s32[21]{0:T(128)S(1)} %concatenate.125.info_ref.refs_0_, f32[1024,768]{1,0:T(8,128)} %copy-done.16, f32[35,768]{1,0:T(8,128)S(1)} %reshape.474.gain_ref, ...), custom_call_target="tpu_custom_call" | custom-call | flops 10000000000 | bytes 20000000 | tf_op jit(solution)/shard_map/forward_rest/pallas_call | solution.py:406
  107.9 4.5 %collective-permute-done.18 = bf16[4,8,2432]{2,1,0:T(8,128)(2,1)S(1)} collective-permute-done((bf16[4,8,2432]{2,1,0:T(8,128)(2,1)S(1)}, bf16[4,8,2432]{2,1,0:T(8,128)(2,1)S(1)}, u32[]{:S(2)}, u32[]{:S(2)}) %collective-permute-start.18) | collective-permute-done | bytes 155680 | tf_op jit(solution)/shard_map/ppermute | solution.py:701
  113.0 6.3 %collective-permute-done.19.a3_ref = bf16[2,4,8,2432]{3,2,1,0:T(8,128)(2,1)S(1)} collective-permute-done((bf16[2,4,8,2432]{3,2,1,0:T(8,128)(2,1)S(1)}, bf16[2,4,8,2432]{3,2,1,0:T(8,128)(2,1)S(1)}, u32[]{:S(2)}, u32[]{:S(2)}) %collective-permute-start.19) | collective-permute-done | bytes 311328 | tf_op jit(solution)/shard_map/ppermute | solution.py:701
  120.9 3.4 %contrast.1 = (f32[1,1]{1,0:T(1,128)}, f32[8,768]{1,0:T(8,128)S(1)}, f32[8,768]{1,0:T(8,128)S(1)}, bf16[256,768]{1,0:T(8,128)(2,1)S(1)}, bf16[256,768]{1,0:T(8,128)(2,1)S(1)}, /*index=5*/f32[1,768]{1,0:T(1,128)S(1)}) custom-call(s32[21]{0:T(128)S(1)} %concatenate.125.info_ref.refs_0_, bf16[2,4,8,2432]{3,2,1,0:T(8,128)(2,1)S(1)} %pad_maximum_fusion.8.a1_ref, ...), custom_call_target="tpu_custom_call" | custom-call | flops 3000000000 | bytes 4000000 | tf_op jit(solution)/shard_map/contrast/pallas_call | solution.py:626
  124.4 16.0 %ffn_back.1 = (f32[1024,768]{1,0:T(8,128)}, bf16[2,768,384]{2,1,0:T(8,128)(2,1)}, f32[8,768]{1,0:T(8,128)S(1)}, bf16[4,1024,128]{2,1,0:T(8,128)(2,1)S(1)}, bf16[...) custom-call(s32[21]{0:T(128)S(1)} %concatenate.125.info_ref.refs_0_, ...), custom_call_target="tpu_custom_call" | custom-call | flops 14000000000 | bytes 20000000 | tf_op jit(solution)/shard_map/ffn_back/pallas_call | solution.py:527
  142.2 16.9 %attend_back.3 = (bf16[4,768,384]{2,1,0:T(8,128)(2,1)}, bf16[4,1024,384]{2,1,0:T(8,128)(2,1)}) custom-call(bf16[768,1024]{1,0:T(8,128)(2,1)S(1)} %copy-done.7, bf16[4,3,1024,128]{3,2,1,0:T(8,128)(2,1)} %get-tuple-element.107.qkv_ref, bf16[4,1024,512]{2,1,0:T(8,128)(2,1)} %get-tuple-element.108.p_ref, bf16[4,1024,128]{2,1,0:T(8,128)(2,1)S(1)} %get-tuple-element.109.aug_ref, ...), custom_call_target="tpu_custom_call" | custom-call | flops 16000000000 | bytes 12000000 | tf_op jit(solution)/shard_map/attend_back/pallas_call | solution.py:212
  165.5 8.8 %attend_back.4 = (bf16[2,768,384]{2,1,0:T(8,128)(2,1)S(1)}, bf16[2,1024,384]{2,1,0:T(8,128)(2,1)S(1)}) custom-call(bf16[768,1024]{1,0:T(8,128)(2,1)S(1)} %copy-done.7, bf16[4,3,1024,128]{3,2,1,0:T(8,128)(2,1)} %get-tuple-element.86.qkv_ref, bf16[4,1024,512]{2,1,0:T(8,128)(2,1)} %get-tuple-element.87.p_ref, bf16[4,1024,128]{2,1,0:T(8,128)(2,1)S(1)} %copy-done.9, ...), custom_call_target="tpu_custom_call" | custom-call | flops 8000000000 | bytes 6000000 | tf_op jit(solution)/shard_map/attend_back/pallas_call | solution.py:212
  179.2 9.0 %attend_back.5 = (bf16[2,2,4,96,384]{4,3,2,1,0:T(8,128)(2,1)S(1)}, bf16[2,1024,384]{2,1,0:T(8,128)(2,1)S(1)}) custom-call(bf16[768,1024]{1,0:T(8,128)(2,1)S(1)} %copy-done.7, bf16[4,3,1024,128]{3,2,1,0:T(8,128)(2,1)} %get-tuple-element.86.qkv_ref, bf16[4,1024,512]{2,1,0:T(8,128)(2,1)} %get-tuple-element.87.p_ref, bf16[4,1024,128]{2,1,0:T(8,128)(2,1)S(1)} %copy-done.10, ...), custom_call_target="tpu_custom_call" | custom-call | flops 8000000000 | bytes 6000000 | tf_op jit(solution)/shard_map/attend_back/pallas_call | solution.py:212
  189.9 4.8 %first_sum.1.sum_ref = f32[1024,768]{1,0:T(8,128)S(1)} custom-call(bf16[4,1024,384]{2,1,0:T(8,128)(2,1)} %get-tuple-element.123.refs_0_, bf16[4,768,384]{2,1,0:T(8,128)(2,1)S(1)} %copy-done.5), custom_call_target="tpu_custom_call" | custom-call | flops 7000000000 | bytes 12000000 | tf_op jit(solution)/shard_map/first_sum/pallas_call | solution.py:252
  194.8 3.6 %collective-permute-done.26 = bf16[2,4,96,384]{3,2,1,0:T(8,128)(2,1)S(1)} collective-permute-done((bf16[2,4,96,384]{3,2,1,0:T(8,128)(2,1)S(1)}, bf16[2,4,96,384]{3,2,1,0:T(8,128)(2,1)S(1)}, u32[]{:S(2)}, u32[]{:S(2)}) %collective-permute-start.26) | collective-permute-done | bytes 589856 | tf_op jit(solution)/shard_map/ppermute | solution.py:701
  201.8 7.1 %first_back.1 = f32[40,768]{1,0:T(8,128)S(1)} custom-call(f32[1024,768]{1,0:T(8,128)} %copy-done.16, f32[1024,768]{1,0:T(8,128)} %get-tuple-element.121.dmid_ref, bf16[1024,32]{1,0:T(8,128)(2,1)S(1)} %copy.82.ident_ref, f32[35,768]{1,0:T(8,128)S(1)} %reshape.474.gain_ref, f32[1024,768]{1,0:T(8,128)} %copy-done.2, ...), custom_call_target="tpu_custom_call" | custom-call | flops 4000000000 | bytes 10000000 | tf_op jit(solution)/shard_map/first_back/pallas_call | solution.py:300
  215.6 3.5 %all-to-all-start.1 = ((f32[32,1,816]{2,1,0:T(1,128)}), f32[32,1,816]{2,1,0:T(1,128)S(1)}, u32[]{:S(2)}, u32[]{:S(2)}) async-start(f32[32,1,816]{2,1,0:T(1,128)} %all_to_all.26), calls=%async_computation.1 | async-start | bytes 229376 | tf_op jit(solution)/shard_map/all_to_all | solution.py:1072
  219.8 5.9 %collective-permute-done.29 = bf16[240,384]{1,0:T(8,128)(2,1)S(1)} collective-permute-done((bf16[240,384]{1,0:T(8,128)(2,1)S(1)}, bf16[240,384]{1,0:T(8,128)(2,1)S(1)}, u32[]{:S(2)}, u32[]{:S(2)}) %collective-permute-start.29) | collective-permute-done | bytes 184352 | tf_op jit(solution)/shard_map/ppermute | solution.py:701
  227.2 4.8 %all-to-all-done.1 = f32[32,1,816]{2,1,0:T(1,128)S(1)} async-done(((f32[32,1,816]{2,1,0:T(1,128)}), f32[32,1,816]{2,1,0:T(1,128)S(1)}, u32[]{:S(2)}, u32[]{:S(2)}) %all-to-all-start.1) | async-done | bytes 104480 | tf_op jit(solution)/shard_map/all_to_all | solution.py:1072
  239.9 4.3 %all-to-all-done.2 = f32[32,1,128]{2,1,0:T(1,128)S(1)} async-done(((f32[32,1,128]{2,1,0:T(1,128)}), f32[32,1,128]{2,1,0:T(1,128)S(1)}, u32[]{:S(2)}, u32[]{:S(2)}) %all-to-all-start.2) | async-done | bytes 16416 | tf_op jit(solution)/shard_map/all_to_all | solution.py:1075
  244.9 3.0 %update.1 = (f32[1,1]{1,0:T(1,128)}, f32[24,32]{1,0:T(8,128)}, f32[3,96,192]{2,1,0:T(8,128)}, f32[192,96]{1,0:T(8,128)}, f32[2,24,768]{2,1,0:T(8,128)}, /*index=...) custom-call(f32[32,128]{1,0:T(8,128)} %bitcast.285, ...), custom_call_target="tpu_custom_call" | custom-call | flops 5000000 | bytes 6000000 | tf_op jit(solution)/shard_map/update/pallas_call | solution.py:896
  (225 shorter events, 83.0 us)
Async XLA Ops:
  4.6 9.7 %collective-permute-start.1 = (bf16[2,96,384]{2,1,0:T(8,128)(2,1)S(1)}, bf16[2,96,384]{2,1,0:T(8,128)(2,1)S(1)}, u32[]{:S(2)}, u32[]{:S(2)}) collective-permute-start(bf16[2,96,384]{2,1,0:T(8,128)(2,1)S(1)} %get-tuple-element.197), channel_id=1, source_target_pairs={{0,8},{1,9},{2,10},{3,11},{4,12},{5,13},{6,14},{7,15},{8,16},{9,17... | collective-permute-start | bytes 442376 | tf_op jit(solution)/shard_map/ppermute | solution.py:701
  7.6 12.6 %collective-permute-start.2 = (bf16[2,96,384]{2,1,0:T(8,128)(2,1)S(1)}, bf16[2,96,384]{2,1,0:T(8,128)(2,1)S(1)}, u32[]{:S(2)}, u32[]{:S(2)}) collective-permute-start(bf16[2,96,384]{2,1,0:T(8,128)(2,1)S(1)} %get-tuple-element.197), channel_id=1, source_target_pairs={{0,16},{1,17},{2,18},{3,19},{4,20},{5,21},{6,22},{7,23},{8,24},{9,... | collective-permute-start | bytes 442376 | tf_op jit(solution)/shard_map/ppermute | solution.py:701
  10.2 10.0 %collective-permute-start.3 = (bf16[2,96,384]{2,1,0:T(8,128)(2,1)S(1)}, bf16[2,96,384]{2,1,0:T(8,128)(2,1)S(1)}, u32[]{:S(2)}, u32[]{:S(2)}) collective-permute-start(bf16[2,96,384]{2,1,0:T(8,128)(2,1)S(1)} %get-tuple-element.197), channel_id=1, source_target_pairs={{0,24},{1,25},{2,26},{3,27},{4,28},{5,29},{6,30},{7,31},{8,0},{9,1... | collective-permute-start | bytes 442376 | tf_op jit(solution)/shard_map/ppermute | solution.py:701
  20.4 17.9 %collective-permute-start.4 = (bf16[4,2,96,384]{3,2,1,0:T(8,128)(2,1)S(1)}, bf16[4,2,96,384]{3,2,1,0:T(8,128)(2,1)S(1)}, u32[]{:S(2)}, u32[]{:S(2)}) collective-permute-start(bf16[4,2,96,384]{3,2,1,0:T(8,128)(2,1)S(1)} %get-tuple-element.178), channel_id=1, source_target_pairs={{0,4},{1,3},{2,6},{3,1},{4,0},{5,7},{6,2},{7,5},{8,12},{9,11},{10,... | collective-permute-start | bytes 1769480 | tf_op jit(solution)/shard_map/ppermute | solution.py:701
  23.4 14.2 %all-to-all-start = ((f32[32,1,840]{2,1,0:T(1,128)}), f32[32,1,840]{2,1,0:T(1,128)S(1)}, u32[]{:S(2)}, u32[]{:S(2)}) async-start(f32[32,1,840]{2,1,0:T(1,128)} %broadcast_in_dim.24), calls=%async_computation | async-start | bytes 229376 | tf_op jit(solution)/shard_map/all_to_all | solution.py:954
  30.1 9.8 %collective-permute-start.9 = (bf16[2,24,768]{2,1,0:T(8,128)(2,1)}, bf16[2,24,768]{2,1,0:T(8,128)(2,1)}, u32[]{:S(2)}, u32[]{:S(2)}) collective-permute-start(bf16[2,24,768]{2,1,0:T(8,128)(2,1)} %pad_maximum_fusion.13), channel_id=1, source_target_pairs={{0,24},{1,25},{2,26},{3,27},{4,28},{5,29},{6,30},{7,31},{8,0},{9,1... | collective-permute-start | bytes 221192 | tf_op jit(solution)/shard_map/ppermute | solution.py:701
  38.4 19.5 %collective-permute-start.5 = (bf16[2,4,2,96,384]{4,3,2,1,0:T(8,128)(2,1)S(1)}, bf16[2,4,2,96,384]{4,3,2,1,0:T(8,128)(2,1)}, u32[]{:S(2)}, u32[]{:S(2)}) collective-permute-start(bf16[2,4,2,96,384]{4,3,2,1,0:T(8,128)(2,1)S(1)} %pad_maximum_fusion.refs_0_), channel_id=1, source_target_pairs={{0,2},{1,5},{2,0},{3,7},{4,6},{5,1},{6,4},{7,3},{8,10},{9,13},{10,... | collective-permute-start | bytes 3538952 | tf_op jit(solution)/shard_map/ppermute | solution.py:701
  38.7 36.6 %collective-permute-start.13 = (bf16[2,4,2,96,384]{4,3,2,1,0:T(8,128)(2,1)S(1)}, bf16[2,4,2,96,384]{4,3,2,1,0:T(8,128)(2,1)}, u32[]{:S(2)}, u32[]{:S(2)}) collective-permute-start(bf16[2,4,2,96,384]{4,3,2,1,0:T(8,128)(2,1)S(1)} %pad_maximum_fusion.refs_0_), channel_id=1, source_target_pairs={{0,1},{1,0},{2,3},{3,2},{4,5},{5,4},{6,7},{7,6},{8,9},{9,8},{10,11... | collective-permute-start | bytes 3538952 | tf_op jit(solution)/shard_map/ppermute | solution.py:701
  44.8 9.9 %collective-permute-start.10 = (bf16[4,2,24,768]{3,2,1,0:T(8,128)(2,1)S(1)}, bf16[4,2,24,768]{3,2,1,0:T(8,128)(2,1)S(1)}, u32[]{:S(2)}, u32[]{:S(2)}) collective-permute-start(bf16[4,2,24,768]{3,2,1,0:T(8,128)(2,1)S(1)} %bitcast_dynamic-update-slice_fusion), channel_id=1, source_target_pairs={{0,4},{1,3},{2,6},{3,1},{4,0},{5,7},{6,2},{7,5},{8,12},{9,11},{10,... | collective-permute-start | bytes 884744 | tf_op jit(solution)/shard_map/ppermute | solution.py:701
  54.8 15.2 %collective-permute-start.11 = (bf16[2,4,2,24,768]{4,3,2,1,0:T(8,128)(2,1)S(1)}, bf16[2,4,2,24,768]{4,3,2,1,0:T(8,128)(2,1)S(1)}, u32[]{:S(2)}, u32[]{:S(2)}) collective-permute-start(bf16[2,4,2,24,768]{4,3,2,1,0:T(8,128)(2,1)S(1)} %pad_maximum_fusion.4), channel_id=1, source_target_pairs={{0,2},{1,5},{2,0},{3,7},{4,6},{5,1},{6,4},{7,3},{8,10},{9,13},{10,... | collective-permute-start | bytes 1769480 | tf_op jit(solution)/shard_map/ppermute | solution.py:701
  57.9 17.5 %collective-permute-start.14 = (bf16[2,4,2,96,384]{4,3,2,1,0:T(8,128)(2,1)}, bf16[2,4,2,96,384]{4,3,2,1,0:T(8,128)(2,1)}, u32[]{:S(2)}, u32[]{:S(2)}) collective-permute-start(bf16[2,4,2,96,384]{4,3,2,1,0:T(8,128)(2,1)} %collective-permute-done.5.refs_1_), channel_id=1, source_target_pairs={{0,1},{1,0},{2,3},{3,2},{4,5},{5,4},{6,7},{7,6},{8,9},{9,8},{10,11... | collective-permute-start | bytes 3538952 | tf_op jit(solution)/shard_map/ppermute | solution.py:701
  72.6 14.4 %collective-permute-start.12 = (bf16[768,768]{1,0:T(8,128)(2,1)}, bf16[768,768]{1,0:T(8,128)(2,1)}, u32[]{:S(2)}, u32[]{:S(2)}) collective-permute-start(bf16[768,768]{1,0:T(8,128)(2,1)} %bitcast.48.ffn_ref), channel_id=1, source_target_pairs={{0,1},{1,0},{2,3},{3,2},{4,5},{5,4},{6,7},{7,6},{8,9},{9,8},{10,11... | collective-permute-start | bytes 3538952 | tf_op jit(solution)/shard_map/ppermute | solution.py:701
  159.1 16.5 %collective-permute-start.22 = (bf16[4,768,384]{2,1,0:T(8,128)(2,1)}, bf16[4,768,384]{2,1,0:T(8,128)(2,1)}, u32[]{:S(2)}, u32[]{:S(2)}) collective-permute-start(bf16[4,768,384]{2,1,0:T(8,128)(2,1)} %get-tuple-element.111), channel_id=1, source_target_pairs={{0,1},{1,0},{2,3},{3,2},{4,5},{5,4},{6,7},{7,6},{8,9},{9,8},{10,11... | collective-permute-start | bytes 7077896 | tf_op jit(solution)/shard_map/ppermute | solution.py:701
  161.9 12.4 %collective-permute-start.23 = (bf16[2,4,2,2,24,384]{5,4,1,3,2,0:T(8,128)(2,1)}, bf16[2,4,2,2,24,384]{5,4,1,3,2,0:T(8,128)(2,1)}, u32[]{:S(2)}, u32[]{:S(2)}) collective-permute-start(bf16[2,4,2,2,24,384]{5,4,1,3,2,0:T(8,128)(2,1)} %bitcast.256), channel_id=1, source_target_pairs={{0,1},{1,0},{2,3},{3,2},{4,5},{5,4},{6,7},{7,6},{8,9},{9,8},{10,11... | collective-permute-start | bytes 1769480 | tf_op jit(solution)/shard_map/ppermute | solution.py:701
  178.7 21.5 %collective-permute-start.24 = (bf16[2,4,144,384]{3,2,1,0:T(8,128)(2,1)}, bf16[2,4,144,384]{3,2,1,0:T(8,128)(2,1)S(1)}, u32[]{:S(2)}, u32[]{:S(2)}) collective-permute-start(bf16[2,4,144,384]{3,2,1,0:T(8,128)(2,1)} %pad_maximum_fusion.2), channel_id=1, source_target_pairs={{0,2},{1,5},{2,0},{3,7},{4,6},{5,1},{6,4},{7,3},{8,10},{9,13},{10,... | collective-permute-start | bytes 2654216 | tf_op jit(solution)/shard_map/ppermute | solution.py:701
  188.4 9.9 %collective-permute-start.26 = (bf16[2,4,96,384]{3,2,1,0:T(8,128)(2,1)S(1)}, bf16[2,4,96,384]{3,2,1,0:T(8,128)(2,1)S(1)}, u32[]{:S(2)}, u32[]{:S(2)}) collective-permute-start(bf16[2,4,96,384]{3,2,1,0:T(8,128)(2,1)S(1)} %pad_maximum_fusion.5), channel_id=1, source_target_pairs={{0,2},{1,5},{2,0},{3,7},{4,6},{5,1},{6,4},{7,3},{8,10},{9,13},{10,... | collective-permute-start | bytes 1769480 | tf_op jit(solution)/shard_map/ppermute | solution.py:701
  198.5 10.4 %collective-permute-start.27 = (bf16[4,96,384]{2,1,0:T(8,128)(2,1)S(1)}, bf16[4,96,384]{2,1,0:T(8,128)(2,1)S(1)}, u32[]{:S(2)}, u32[]{:S(2)}) collective-permute-start(bf16[4,96,384]{2,1,0:T(8,128)(2,1)S(1)} %fusion.12), channel_id=1, source_target_pairs={{0,4},{1,3},{2,6},{3,1},{4,0},{5,7},{6,2},{7,5},{8,12},{9,11},{10,... | collective-permute-start | bytes 884744 | tf_op jit(solution)/shard_map/ppermute | solution.py:701
  200.4 9.7 %collective-permute-start.25 = (bf16[4,144,384]{2,1,0:T(8,128)(2,1)S(1)}, bf16[4,144,384]{2,1,0:T(8,128)(2,1)S(1)}, u32[]{:S(2)}, u32[]{:S(2)}) collective-permute-start(bf16[4,144,384]{2,1,0:T(8,128)(2,1)S(1)} %fusion.5), channel_id=1, source_target_pairs={{0,4},{1,3},{2,6},{3,1},{4,0},{5,7},{6,2},{7,5},{8,12},{9,11},{10,... | collective-permute-start | bytes 1327112 | tf_op jit(solution)/shard_map/ppermute | solution.py:701
  210.3 9.5 %collective-permute-start.28 = (bf16[240,384]{1,0:T(8,128)(2,1)S(1)}, bf16[240,384]{1,0:T(8,128)(2,1)S(1)}, u32[]{:S(2)}, u32[]{:S(2)}) collective-permute-start(bf16[240,384]{1,0:T(8,128)(2,1)S(1)} %get-tuple-element.162), channel_id=1, source_target_pairs={{0,8},{1,9},{2,10},{3,11},{4,12},{5,13},{6,14},{7,15},{8,16},{9,17... | collective-permute-start | bytes 552968 | tf_op jit(solution)/shard_map/ppermute | solution.py:701
  212.0 13.7 %collective-permute-start.29 = (bf16[240,384]{1,0:T(8,128)(2,1)S(1)}, bf16[240,384]{1,0:T(8,128)(2,1)S(1)}, u32[]{:S(2)}, u32[]{:S(2)}) collective-permute-start(bf16[240,384]{1,0:T(8,128)(2,1)S(1)} %get-tuple-element.163), channel_id=1, source_target_pairs={{0,16},{1,17},{2,18},{3,19},{4,20},{5,21},{6,22},{7,23},{8,24},{9,... | collective-permute-start | bytes 552968 | tf_op jit(solution)/shard_map/ppermute | solution.py:701
  213.8 11.8 %collective-permute-start.30 = (bf16[240,384]{1,0:T(8,128)(2,1)S(1)}, bf16[240,384]{1,0:T(8,128)(2,1)S(1)}, u32[]{:S(2)}, u32[]{:S(2)}) collective-permute-start(bf16[240,384]{1,0:T(8,128)(2,1)S(1)} %get-tuple-element.164), channel_id=1, source_target_pairs={{0,24},{1,25},{2,26},{3,27},{4,28},{5,29},{6,30},{7,31},{8,0},{9,1... | collective-permute-start | bytes 552968 | tf_op jit(solution)/shard_map/ppermute | solution.py:701
  215.6 16.4 %all-to-all-start.1 = ((f32[32,1,816]{2,1,0:T(1,128)}), f32[32,1,816]{2,1,0:T(1,128)S(1)}, u32[]{:S(2)}, u32[]{:S(2)}) async-start(f32[32,1,816]{2,1,0:T(1,128)} %all_to_all.26), calls=%async_computation.1 | async-start | bytes 229376 | tf_op jit(solution)/shard_map/all_to_all | solution.py:1072
  225.8 12.0 %collective-permute-start.31 = (f32[96,384]{1,0:T(8,128)S(1)}, f32[96,384]{1,0:T(8,128)S(1)}, u32[]{:S(2)}, u32[]{:S(2)}) collective-permute-start(f32[96,384]{1,0:T(8,128)S(1)} %slice.268.refs_1_), channel_id=1, source_target_pairs={{0,1},{1,0},{2,3},{3,2},{4,5},{5,4},{6,7},{7,6},{8,9},{9,8},{10,11... | collective-permute-start | bytes 442376 | tf_op jit(solution)/shard_map/ppermute | solution.py:701
  234.6 9.6 %all-to-all-start.2 = ((f32[32,1,128]{2,1,0:T(1,128)}), f32[32,1,128]{2,1,0:T(1,128)S(1)}, u32[]{:S(2)}, u32[]{:S(2)}) async-start(f32[32,1,128]{2,1,0:T(1,128)} %bitcast.286), calls=%async_computation.2 | async-start | bytes 32768 | tf_op jit(solution)/shard_map/all_to_all | solution.py:1075
  (41 other events, 351.6 us)
